TPU v7x, 128 devices: a whole 4x4x4 slice. The times are simulated.
128 devices in a mesh: gz: 32 (over x, z, core), gy: 4 (over y).
Axes of the slice: x: 4, y: 4, z: 4, core: 2. Of those that a mesh axis runs over, the one named last changes fastest.
Arguments:
- features: bfloat16 [512, 64, 32, 128], P('gz', 'gy'), may hold values from -6 to 6
- occupancy: int32 [32, 4, 4], P('gz', 'gy'), may hold values from 0 to 1, as said below
- kernel: bfloat16 [3, 3, 3, 64, 128], replicated, may hold values from -0.15625 to 0.15625
- upstream: bfloat16 [256, 32, 32, 128], P('gz', 'gy'), may hold values from -6 to 6
Outputs:
- coarse: bfloat16 [256, 32, 32, 128], P('gz', 'gy')
- feature_grad: bfloat16 [512, 64, 32, 128], P('gz', 'gy')
- kernel_grad: float32 [3, 3, 3, 64, 128], replicated
Inputs may be any that keep to these rules, and one draw needn't show every extreme that they name: `occupancy`: each owner of 1 x 1 x 4 blocks holds at least one occupied block; owners' blocks are occupied at their own rates, so occupied counts differ between devices.
All inputs are finite; a program needn't handle non-finite values.
Results may differ from a plain program's by a relative error of at most 0.0022.
Values may be sent and summed in bfloat16 or wider, within the bound.
A program may use at most 128 MiB of HBM per device.

v0:
```python
import jax
import jax.numpy as jnp
from jax import lax
from jax.experimental import pallas as pl
from jax.experimental.pallas import tpu as pltpu
from jax.sharding import PartitionSpec as P

MESH = pl.DeviceIdType.MESH
F32 = jnp.float32
BF16 = jnp.bfloat16
HALF = 864
CHUNK = 16
PEERS = 63


def coordinates():
    gz, gy = lax.axis_index("gz"), lax.axis_index("gy")
    return gz // 8, gy, (gz // 2) % 4, gz % 2


def far_first(t):
    return jnp.where(t == 0, 2, jnp.where(t == 1, 1, jnp.where(t == 2, 3, 0)))


def peer(k, sign):
    x, y, z, c = coordinates()
    px = (x + sign * far_first(k // 16) + 4) % 4
    py = (y + sign * far_first((k // 4) % 4) + 4) % 4
    pz = (z + sign * far_first(k % 4) + 4) % 4
    return px * 16 + py * 4 + pz, ((px * 4 + pz) * 2 + c, py)


def chunk_row(j):
    return ((j * 106) // 63) * 8


def remote(src, dst, send, recv, device):
    return pltpu.make_async_remote_copy(
        src_ref=src, dst_ref=dst, send_sem=send, recv_sem=recv, device_id=device, device_id_type=MESH
    )


def kernel_body(
    feat, occ, ker, ups, coarse, fgrad, kgrad,
    fv, gp, wv, mask, wide, gwt, wf, wd, acc,
    fz_s, fy_s, fz_r, fy_r, fc_r, gz_r, gy_r, gc_r,
    pair_r, rs_r, ag, ag_x, co_v, fg_v, kg_v,
    in_sem, hs_sem, hr_sem, pair_sem, rs_sem, ag_sem, out_sem,
):
    gz, gy = lax.axis_index("gz"), lax.axis_index("gy")
    x, y, z, c = coordinates()
    me = x * 16 + y * 4 + z
    other = (gz + 1 - 2 * c, gy)
    up, down = (gz + 1) % 32, (gz + 31) % 32
    nxt, prv = (gy + 1) % 4, (gy + 3) % 4

    copies = [
        pltpu.make_async_copy(ups, gp.at[0:8, 0:8], in_sem.at[0]),
        pltpu.make_async_copy(feat, fv, in_sem.at[1]),
        pltpu.make_async_copy(ker, wv, in_sem.at[2]),
    ]
    for copy in copies:
        copy.start()

    barrier = pltpu.get_barrier_semaphore()
    for device in ((up, gy), (down, gy), (gz, nxt), (gz, prv), (up, nxt), (down, prv)):
        pl.semaphore_signal(barrier, inc=1, device_id=device, device_id_type=MESH)

    def greet(k, _):
        pl.semaphore_signal(barrier, inc=1, device_id=peer(k, 1)[1], device_id_type=MESH)
        return 0

    lax.fori_loop(0, PEERS, greet, 0)

    pair = lax.broadcasted_iota(jnp.int32, (256, 128), 0) % 32
    held = jnp.zeros((256, 128), jnp.int32)
    for k in range(4):
        held = jnp.where(pair // 8 == k, occ[0, 0, k], held)
    mask[...] = held.astype(F32)
    m32 = held.astype(F32)[:32].astype(BF16)

    copies[2].wait()
    for tap in range(9):
        kz, ky = tap // 3, tap % 3
        rows = slice(tap * 128, tap * 128 + 128)
        left = jnp.concatenate([wv[kz, ky, 1], wv[kz, ky, 2]], 0)
        right = jnp.concatenate([jnp.zeros((64, 128), BF16), wv[kz, ky, 0]], 0)
        wf[rows, 0:128] = left
        wf[rows, 128:256] = right
        wd[rows, 0:128] = left.astype(F32).T.astype(BF16)
        wd[rows, 128:256] = right.astype(F32).T.astype(BF16)

    copies[0].wait()

    def mask_grad(a, _):
        held_g = gp[a, 0:8] * m32[None]
        gp[a, 0:8] = held_g
        flat = held_g.reshape(256, 128).astype(F32)
        later = jnp.where(pair == 31, 0.0, pltpu.roll(flat, 255, 0))
        lanes = pl.ds(pl.multiple_of(a * 256, 256), 256)
        gwt[0:128, lanes] = flat.T.astype(BF16)
        gwt[128:256, lanes] = later.T.astype(BF16)
        return 0

    lax.fori_loop(0, 8, mask_grad, 0)

    copies[1].wait()
    fz_s[...] = fv[15] * m32[None]
    fy_s[...] = fv[:, 15] * m32[None]

    def widen(a, first):
        for kz in range(3):
            for ky in range(3):
                for b in range(8):
                    if (first and kz == 0) or (ky == 0 and b == 0):
                        continue
                    rows = pl.ds(pl.multiple_of(a * 256 + b * 32, 32), 32)
                    tap = kz * 3 + ky
                    wide[rows, tap * 128 : tap * 128 + 128] = fv[2 * a - 1 + kz, 2 * b - 1 + ky] * m32

    widen(0, True)

    def widen_later(a, _):
        widen(a, False)
        return 0

    lax.fori_loop(1, 8, widen_later, 0)

    pl.semaphore_wait(barrier, 6 + PEERS)

    halos = [
        remote(fz_s, fz_r, hs_sem.at[0], hr_sem.at[0], (up, gy)),
        remote(fy_s, fy_r, hs_sem.at[1], hr_sem.at[1], (gz, nxt)),
        remote(fz_s.at[15], fc_r, hs_sem.at[2], hr_sem.at[2], (up, nxt)),
        remote(gp.at[0, 0:8], gz_r, hs_sem.at[3], hr_sem.at[3], (down, gy)),
        remote(gp.at[0:8, 0], gy_r, hs_sem.at[4], hr_sem.at[4], (gz, prv)),
        remote(gp.at[0, 0], gc_r, hs_sem.at[5], hr_sem.at[5], (down, prv)),
    ]
    for copy in halos:
        copy.start()
    for copy in halos[:3]:
        copy.wait_recv()

    has_z = jnp.where(gz > 0, 1.0, 0.0) * jnp.ones((32, 128), F32)
    has_y = jnp.where(gy > 0, 1.0, 0.0) * jnp.ones((32, 128), F32)
    z_on, y_on, c_on = has_z.astype(BF16), has_y.astype(BF16), (has_z * has_y).astype(BF16)
    for ky in range(3):
        for b in range(8):
            row = 2 * b - 1 + ky
            rim = fc_r[...] * c_on if row < 0 else fz_r[row] * z_on
            wide[b * 32 : b * 32 + 32, ky * 128 : ky * 128 + 128] = rim
    for a in range(8):
        for kz in range(3):
            plane = 2 * a - 1 + kz
            if plane >= 0:
                wide[a * 256 : a * 256 + 32, kz * 384 : kz * 384 + 128] = fy_r[plane] * y_on

    for first in range(0, 9, 2):
        taps = range(first, min(first + 2, 9))
        out = jnp.dot(
            gwt[...], wide[:, first * 128 : (taps[-1] + 1) * 128], preferred_element_type=F32
        )
        for tap in taps:
            piece = out[:, (tap - first) * 128 : (tap - first) * 128 + 128]
            acc[tap * 192 + 64 : tap * 192 + 192] = piece[:128].T
            acc[tap * 192 : tap * 192 + 64] = piece[128:].T[64:]

    mine = pl.multiple_of(c * HALF, 8)
    theirs = pl.multiple_of((1 - c) * HALF, 8)
    swap = remote(acc.at[pl.ds(theirs, HALF)], pair_r, pair_sem.at[0], pair_sem.at[1], other)
    swap.start()
    swap.wait_recv()
    acc[pl.ds(mine, HALF)] = acc[pl.ds(mine, HALF)] + pair_r[...]

    def scatter(k, _):
        j, device = peer(k, 1)
        row = pl.multiple_of(c * HALF + chunk_row(j), 8)
        remote(acc.at[pl.ds(row, CHUNK)], rs_r.at[k], rs_sem.at[0], rs_sem.at[1], device).start()
        return 0

    lax.fori_loop(0, PEERS, scatter, 0)

    for copy in halos[3:]:
        copy.wait_recv()
    for copy in halos:
        copy.wait_send()
    last_z = (jnp.where(gz < 31, 1.0, 0.0) * jnp.ones((32, 128), F32))
    last_y = (jnp.where(gy < 3, 1.0, 0.0) * jnp.ones((32, 128), F32))
    gp[8, 0:8] = gz_r[...] * last_z.astype(BF16)[None]
    gp[0:8, 8] = gy_r[...] * last_y.astype(BF16)[None]
    gp[8, 8] = gc_r[...] * (last_z * last_y).astype(BF16)

    def tap_rows(kz, ky):
        return wd[(kz * 3 + ky) * 128 : (kz * 3 + ky) * 128 + 128]

    def back(a, _):
        here = [gp[a + i, j : j + 8].reshape(256, 128) for i in range(2) for j in range(2)]
        for ez in range(2):
            for ey in range(2):
                lhs, rhs = [], []
                for i in range(1 + ez):
                    for j in range(1 + ey):
                        kz = 1 if ez == 0 else 2 - 2 * i
                        ky = 1 if ey == 0 else 2 - 2 * j
                        lhs.append(here[i * 2 + j])
                        rhs.append(tap_rows(kz, ky))
                d = jnp.dot(
                    jnp.concatenate(lhs, 1), jnp.concatenate(rhs, 0), preferred_element_type=F32
                )
                late = jnp.where(pair == 31, 0.0, pltpu.roll(d[:, 128:], 255, 0))
                out = ((d[:, :128] + late) * mask[...]).astype(BF16)
                for b in range(8):
                    fg_v[2 * a + ez, 2 * b + ey] = out[b * 32 : b * 32 + 32]
        return 0

    lax.fori_loop(0, 8, back, 0)
    fg_out = pltpu.make_async_copy(fg_v, fgrad, out_sem.at[0])
    fg_out.start()

    pltpu.make_async_copy(rs_r, rs_r, rs_sem.at[1]).wait()
    own = acc[pl.ds(pl.multiple_of(c * HALF + chunk_row(me), 8), CHUNK)]
    total = lax.fori_loop(0, PEERS, lambda k, t: t + rs_r[k], own)
    ag[me] = total.astype(BF16)

    def gather(k, _):
        remote(ag.at[me], ag.at[me], ag_sem.at[0], ag_sem.at[1], peer(k, 1)[1]).start()
        return 0

    lax.fori_loop(0, PEERS, gather, 0)

    def forward(a, _):
        rows = pl.ds(pl.multiple_of(a * 256, 256), 256)
        d = jnp.dot(wide[rows, :], wf[...], preferred_element_type=F32)
        late = jnp.where(pair == 0, 0.0, pltpu.roll(d[:, 128:], 1, 0))
        co_v[a] = ((d[:, :128] + late) * mask[...]).astype(BF16).reshape(8, 32, 128)
        return 0

    lax.fori_loop(0, 8, forward, 0)
    co_out = pltpu.make_async_copy(co_v, coarse, out_sem.at[1])
    co_out.start()

    pltpu.make_async_copy(ag.at[0:PEERS], ag.at[0:PEERS], ag_sem.at[1]).wait()
    trade = remote(ag, ag_x, pair_sem.at[2], pair_sem.at[3], other)
    trade.start()

    def place(buffer, base):
        def put(j, _):
            row = pl.multiple_of(base + chunk_row(j), 8)
            kg_v[pl.ds(row, CHUNK)] = buffer[j].astype(F32)
            return 0

        lax.fori_loop(0, 64, put, 0)

    place(ag, mine)
    trade.wait_recv()
    place(ag_x, theirs)
    kg_out = pltpu.make_async_copy(kg_v, kgrad, out_sem.at[2])
    kg_out.start()

    swap.wait_send()
    trade.wait_send()
    pltpu.make_async_copy(rs_r, rs_r, rs_sem.at[0]).wait()
    pltpu.make_async_copy(ag.at[0:PEERS], ag.at[0:PEERS], ag_sem.at[0]).wait()
    fg_out.wait()
    co_out.wait()
    kg_out.wait()


def shards(features, occupancy, kernel, upstream):
    vm = pltpu.VMEM
    dma = pltpu.SemaphoreType.DMA
    any_space = pl.BlockSpec(memory_space=pl.ANY)
    coarse, fgrad, kgrad = pl.pallas_call(
        kernel_body,
        out_shape=(
            jax.ShapeDtypeStruct((8, 8, 32, 128), BF16),
            jax.ShapeDtypeStruct((16, 16, 32, 128), BF16),
            jax.ShapeDtypeStruct((1728, 128), F32),
        ),
        in_specs=[any_space, pl.BlockSpec(memory_space=pltpu.SMEM), any_space, any_space],
        out_specs=(any_space, any_space, any_space),
        scratch_shapes=[
            vm((16, 16, 32, 128), BF16),
            vm((9, 9, 32, 128), BF16),
            vm((3, 3, 3, 64, 128), BF16),
            vm((256, 128), F32),
            vm((2048, 1152), BF16),
            vm((256, 2048), BF16),
            vm((1152, 256), BF16),
            vm((1152, 256), BF16),
            vm((1728, 128), F32),
            vm((16, 32, 128), BF16),
            vm((16, 32, 128), BF16),
            vm((16, 32, 128), BF16),
            vm((16, 32, 128), BF16),
            vm((32, 128), BF16),
            vm((8, 32, 128), BF16),
            vm((8, 32, 128), BF16),
            vm((32, 128), BF16),
            vm((HALF, 128), F32),
            vm((PEERS, CHUNK, 128), F32),
            vm((64, CHUNK, 128), BF16),
            vm((64, CHUNK, 128), BF16),
            vm((8, 8, 32, 128), BF16),
            vm((16, 16, 32, 128), BF16),
            vm((1728, 128), F32),
            dma((3,)),
            dma((6,)),
            dma((6,)),
            dma((4,)),
            dma((2,)),
            dma((2,)),
            dma((3,)),
        ],
        compiler_params=pltpu.CompilerParams(
            collective_id=0, has_side_effects=True, vmem_limit_bytes=48 * 1024 * 1024
        ),
    )(features, occupancy, kernel, upstream)
    return coarse, fgrad, kgrad.reshape(3, 3, 3, 64, 128)


def solution(mesh):
    whole = P("gz", "gy", None, None)
    return jax.shard_map(
        shards,
        mesh=mesh,
        in_specs=(whole, P("gz", "gy", None), P(), whole),
        out_specs=(whole, whole, P()),
        check_vma=False,
    )
```

profile of v0, /device:TPU:1, one launch (start us, length us, event | category | flops | bytes accessed | tf_op | source)
XLA Modules:
  0.0 47.0 jit_solution(15542592462171616897)
XLA Ops:
  0.6 0.0 copy-start
  0.6 1.0 %copy-done = bf16[8,8,32,128]{3,2,1,0:T(8,128)(2,1)S(1)} copy-done((bf16[8,8,32,128]{3,2,1,0:T(8,128)(2,1)S(1)}, bf16[8,8,32,128]{3,2,1,0:T(8,128)(2,1)}, u32[]{:S(2)}) %copy-start) | copy-done | bytes 524312
  1.7 0.0 copy-start.1
  1.7 1.0 %copy-done.1 = bf16[3,3,3,64,128]{4,3,2,1,0:T(8,128)(2,1)S(1)} copy-done((bf16[3,3,3,64,128]{4,3,2,1,0:T(8,128)(2,1)S(1)}, bf16[3,3,3,64,128]{4,3,2,1,0:T(8,128)(2,1)}, u32[]{:S(2)}) %copy-start.1) | copy-done | bytes 442392
  2.7 0.0 copy-start.2
  2.7 0.7 %copy-done.2 = s32[1,1,4]{2,1,0:T(1,128)S(1)} copy-done((s32[1,1,4]{2,1,0:T(1,128)S(1)}, s32[1,1,4]{2,1,0:T(1,128)}, u32[]{:S(2)}) %copy-start.2) | copy-done | bytes 40
  3.3 40.6 %shard_map.67 = (bf16[8,8,32,128]{3,2,1,0:T(8,128)(2,1)S(1)}, bf16[16,16,32,128]{3,2,1,0:T(8,128)(2,1)S(1)}, f32[1728,128]{1,0:T(8,128)S(1)}) custom-call(bf16[16,16,32,128]{3,2,1,0:T(8,128)(2,1)} %feat.1, s32[1,1,4]{2,1,0:T(1,128)S(1)} %copy-done.2, bf16[3,3,3,64,128]{4,3,2,1,0:T(8,128)(2,1)S(1)} %copy-done.1, bf16[8,8,32,128]{3,2,1,0:T(8,128)(2,1)S(1)} %copy-done), custom_call_target="tpu_custom_call" | custom-call | tf_op jit(solution)/shard_map/pallas_call | solution.py:273
  43.9 0.8 %copy.10 = bf16[8,8,32,128]{3,2,1,0:T(8,128)(2,1)} copy(bf16[8,8,32,128]{3,2,1,0:T(8,128)(2,1)S(1)} %get-tuple-element.12) | data formatting | bytes 1048576
  44.7 1.3 %copy.11 = bf16[16,16,32,128]{3,2,1,0:T(8,128)(2,1)} copy(bf16[16,16,32,128]{3,2,1,0:T(8,128)(2,1)S(1)} %get-tuple-element.13) | data formatting | bytes 4194304
  46.1 0.9 %copy.12 = f32[3,3,3,64,128]{4,3,2,1,0:T(8,128)} copy(f32[3,3,3,64,128]{4,3,2,1,0:T(8,128)S(1)} %bitcast.1) | data formatting | bytes 1769472
Async XLA Ops:
  0.6 1.0 %copy-start = (bf16[8,8,32,128]{3,2,1,0:T(8,128)(2,1)S(1)}, bf16[8,8,32,128]{3,2,1,0:T(8,128)(2,1)}, u32[]{:S(2)}) copy-start(bf16[8,8,32,128]{3,2,1,0:T(8,128)(2,1)} %ups.1) | copy-start | bytes 1572868
  1.7 1.0 %copy-start.1 = (bf16[3,3,3,64,128]{4,3,2,1,0:T(8,128)(2,1)S(1)}, bf16[3,3,3,64,128]{4,3,2,1,0:T(8,128)(2,1)}, u32[]{:S(2)}) copy-start(bf16[3,3,3,64,128]{4,3,2,1,0:T(8,128)(2,1)} %ker.1) | copy-start | bytes 1327108
  2.7 0.7 %copy-start.2 = (s32[1,1,4]{2,1,0:T(1,128)S(1)}, s32[1,1,4]{2,1,0:T(1,128)}, u32[]{:S(2)}) copy-start(s32[1,1,4]{2,1,0:T(1,128)} %occ.1) | copy-start | bytes 52
where the time goes:
time: 47.2 us; the launch traced here: 47 us
  Pallas kernels  40.6 us (86%)
  local copies, waits for them, and re-layouts  5.73 us (12%)
  between operations  0.65 us (1%)
    pallas_call x1, Pallas kernels, shards(): pl.pallas_call(kernel_body, out_shape=(jax.ShapeDtypeStruct((8, 8, 32, 12...  40.6 us
    unnamed x9, local copies, waits for them, and re-layouts  5.73 us

commit v1 on v0

--- a/solution.py
+++ b/solution.py
@@ -45,7 +45,7 @@
     fv, gp, wv, mask, wide, gwt, wf, wd, acc,
     fz_s, fy_s, fz_r, fy_r, fc_r, gz_r, gy_r, gc_r,
     pair_r, rs_r, ag, ag_x, co_v, fg_v, kg_v,
-    in_sem, hs_sem, hr_sem, pair_sem, rs_sem, ag_sem, out_sem,
+    gwy, rim_y, know, in_sem, hs_sem, hr_sem, pair_sem, rs_sem, ag_sem, out_sem,
 ):
     gz, gy = lax.axis_index("gz"), lax.axis_index("gy")
     x, y, z, c = coordinates()
@@ -63,14 +63,12 @@
         copy.start()
 
     barrier = pltpu.get_barrier_semaphore()
-    for device in ((up, gy), (down, gy), (gz, nxt), (gz, prv), (up, nxt), (down, prv)):
+    along_x = [((((x + i) % 4) * 4 + z) * 2 + c, gy) for i in (2, 1, 3)]
+    along_y = [(gz, (gy + i) % 4) for i in (2, 1, 3)]
+    along_z = [((x * 4 + (z + i) % 4) * 2 + c, gy) for i in (2, 1, 3)]
+    beside = [(up, nxt), (down, prv), (up, gy), (down, gy)]
+    for device in beside + along_y + along_x + along_z:
         pl.semaphore_signal(barrier, inc=1, device_id=device, device_id_type=MESH)
-
-    def greet(k, _):
-        pl.semaphore_signal(barrier, inc=1, device_id=peer(k, 1)[1], device_id_type=MESH)
-        return 0
-
-    lax.fori_loop(0, PEERS, greet, 0)
 
     pair = lax.broadcasted_iota(jnp.int32, (256, 128), 0) % 32
     held = jnp.zeros((256, 128), jnp.int32)
@@ -79,54 +77,18 @@
     mask[...] = held.astype(F32)
     m32 = held.astype(F32)[:32].astype(BF16)
 
-    copies[2].wait()
-    for tap in range(9):
-        kz, ky = tap // 3, tap % 3
-        rows = slice(tap * 128, tap * 128 + 128)
-        left = jnp.concatenate([wv[kz, ky, 1], wv[kz, ky, 2]], 0)
-        right = jnp.concatenate([jnp.zeros((64, 128), BF16), wv[kz, ky, 0]], 0)
-        wf[rows, 0:128] = left
-        wf[rows, 128:256] = right
-        wd[rows, 0:128] = left.astype(F32).T.astype(BF16)
-        wd[rows, 128:256] = right.astype(F32).T.astype(BF16)
-
     copies[0].wait()
 
     def mask_grad(a, _):
-        held_g = gp[a, 0:8] * m32[None]
-        gp[a, 0:8] = held_g
-        flat = held_g.reshape(256, 128).astype(F32)
-        later = jnp.where(pair == 31, 0.0, pltpu.roll(flat, 255, 0))
-        lanes = pl.ds(pl.multiple_of(a * 256, 256), 256)
-        gwt[0:128, lanes] = flat.T.astype(BF16)
-        gwt[128:256, lanes] = later.T.astype(BF16)
+        gp[a, 0:8] = gp[a, 0:8] * m32[None]
         return 0
 
     lax.fori_loop(0, 8, mask_grad, 0)
-
     copies[1].wait()
     fz_s[...] = fv[15] * m32[None]
     fy_s[...] = fv[:, 15] * m32[None]
 
-    def widen(a, first):
-        for kz in range(3):
-            for ky in range(3):
-                for b in range(8):
-                    if (first and kz == 0) or (ky == 0 and b == 0):
-                        continue
-                    rows = pl.ds(pl.multiple_of(a * 256 + b * 32, 32), 32)
-                    tap = kz * 3 + ky
-                    wide[rows, tap * 128 : tap * 128 + 128] = fv[2 * a - 1 + kz, 2 * b - 1 + ky] * m32
-
-    widen(0, True)
-
-    def widen_later(a, _):
-        widen(a, False)
-        return 0
-
-    lax.fori_loop(1, 8, widen_later, 0)
-
-    pl.semaphore_wait(barrier, 6 + PEERS)
+    pl.semaphore_wait(barrier, 13)
 
     halos = [
         remote(fz_s, fz_r, hs_sem.at[0], hr_sem.at[0], (up, gy)),
@@ -138,6 +100,57 @@
     ]
     for copy in halos:
         copy.start()
+    for device in along_y:
+        pl.semaphore_signal(know.at[0], inc=1, device_id=device, device_id_type=MESH)
+
+    def turn(rows, ref, first):
+        flat = rows.reshape(256, 128).astype(F32)
+        later = jnp.where(pair == 31, 0.0, pltpu.roll(flat, 255, 0))
+        lanes = pl.ds(first if isinstance(first, int) else pl.multiple_of(first, 256), 256)
+        ref[0:128, lanes] = flat.T.astype(BF16)
+        ref[128:256, lanes] = later.T.astype(BF16)
+
+    def turn_plane(a, _):
+        turn(gp[a, 0:8], gwt, a * 256)
+        return 0
+
+    lax.fori_loop(0, 8, turn_plane, 0)
+    turn(gp[0:8, 0], gwy, 0)
+
+    def widen(a, first):
+        for kz in range(3):
+            for ky in range(3):
+                tap = kz * 3 + ky
+                for b in range(8):
+                    rows = pl.ds(pl.multiple_of(a * 256 + b * 32, 32), 32)
+                    if (first and kz == 0) or (ky == 0 and b == 0):
+                        piece = jnp.zeros((32, 128), BF16)
+                    else:
+                        piece = fv[2 * a - 1 + kz, 2 * b - 1 + ky] * m32
+                    wide[rows, tap * 128 : tap * 128 + 128] = piece
+
+    widen(0, True)
+
+    def widen_later(a, _):
+        widen(a, False)
+        return 0
+
+    lax.fori_loop(1, 8, widen_later, 0)
+
+    for first in range(0, 9, 2):
+        taps = range(first, min(first + 2, 9))
+        out = jnp.dot(
+            gwt[...], wide[:, first * 128 : (taps[-1] + 1) * 128], preferred_element_type=F32
+        )
+        for tap in taps:
+            piece = out[:, (tap - first) * 128 : (tap - first) * 128 + 128]
+            acc[tap * 192 + 64 : tap * 192 + 192] = piece[:128].T
+            acc[tap * 192 : tap * 192 + 64] = piece[128:].T[64:]
+
+    pl.semaphore_wait(know.at[0], 3)
+    for device in along_x:
+        pl.semaphore_signal(know.at[1], inc=1, device_id=device, device_id_type=MESH)
+
     for copy in halos[:3]:
         copy.wait_recv()
 
@@ -152,18 +165,17 @@
     for a in range(8):
         for kz in range(3):
             plane = 2 * a - 1 + kz
+            rim = fy_r[plane] * y_on if plane >= 0 else jnp.zeros((32, 128), BF16)
+            rim_y[a * 32 : a * 32 + 32, kz * 128 : kz * 128 + 128] = rim
             if plane >= 0:
-                wide[a * 256 : a * 256 + 32, kz * 384 : kz * 384 + 128] = fy_r[plane] * y_on
-
-    for first in range(0, 9, 2):
-        taps = range(first, min(first + 2, 9))
-        out = jnp.dot(
-            gwt[...], wide[:, first * 128 : (taps[-1] + 1) * 128], preferred_element_type=F32
-        )
-        for tap in taps:
-            piece = out[:, (tap - first) * 128 : (tap - first) * 128 + 128]
-            acc[tap * 192 + 64 : tap * 192 + 192] = piece[:128].T
-            acc[tap * 192 : tap * 192 + 64] = piece[128:].T[64:]
+                wide[a * 256 : a * 256 + 32, kz * 384 : kz * 384 + 128] = rim
+    by_z = jnp.dot(gwt[:, 0:256], wide[0:256, 0:384], preferred_element_type=F32)
+    by_y = jnp.dot(gwy[...], rim_y[...], preferred_element_type=F32)
+    for tap, terms in ((0, by_z), (1, by_z), (2, by_z), (0, by_y), (3, by_y), (6, by_y)):
+        at = tap if terms is by_z else tap // 3
+        piece = terms[:, at * 128 : at * 128 + 128]
+        acc[tap * 192 + 64 : tap * 192 + 192] += piece[:128].T
+        acc[tap * 192 : tap * 192 + 64] += piece[128:].T[64:]
 
     mine = pl.multiple_of(c * HALF, 8)
     theirs = pl.multiple_of((1 - c) * HALF, 8)
@@ -172,6 +184,8 @@
     swap.wait_recv()
     acc[pl.ds(mine, HALF)] = acc[pl.ds(mine, HALF)] + pair_r[...]
 
+    pl.semaphore_wait(know.at[1], 3)
+
     def scatter(k, _):
         j, device = peer(k, 1)
         row = pl.multiple_of(c * HALF + chunk_row(j), 8)
@@ -179,6 +193,17 @@
         return 0
 
     lax.fori_loop(0, PEERS, scatter, 0)
+
+    copies[2].wait()
+    for tap in range(9):
+        kz, ky = tap // 3, tap % 3
+        rows = slice(tap * 128, tap * 128 + 128)
+        left = jnp.concatenate([wv[kz, ky, 1], wv[kz, ky, 2]], 0)
+        right = jnp.concatenate([jnp.zeros((64, 128), BF16), wv[kz, ky, 0]], 0)
+        wf[rows, 0:128] = left
+        wf[rows, 128:256] = right
+        wd[rows, 0:128] = left.astype(F32).T.astype(BF16)
+        wd[rows, 128:256] = right.astype(F32).T.astype(BF16)
 
     for copy in halos[3:]:
         copy.wait_recv()
@@ -270,6 +295,7 @@
     vm = pltpu.VMEM
     dma = pltpu.SemaphoreType.DMA
     any_space = pl.BlockSpec(memory_space=pl.ANY)
+    hbm = pl.BlockSpec(memory_space=pltpu.HBM)
     coarse, fgrad, kgrad = pl.pallas_call(
         kernel_body,
         out_shape=(
@@ -277,7 +303,7 @@
             jax.ShapeDtypeStruct((16, 16, 32, 128), BF16),
             jax.ShapeDtypeStruct((1728, 128), F32),
         ),
-        in_specs=[any_space, pl.BlockSpec(memory_space=pltpu.SMEM), any_space, any_space],
+        in_specs=[hbm, pl.BlockSpec(memory_space=pltpu.SMEM), hbm, hbm],
         out_specs=(any_space, any_space, any_space),
         scratch_shapes=[
             vm((16, 16, 32, 128), BF16),
@@ -304,6 +330,9 @@
             vm((8, 8, 32, 128), BF16),
             vm((16, 16, 32, 128), BF16),
             vm((1728, 128), F32),
+            vm((256, 256), BF16),
+            vm((256, 384), BF16),
+            pltpu.SemaphoreType.REGULAR((2,)),
             dma((3,)),
             dma((6,)),
             dma((6,)),

time: 47.2 us -> 43.1 us (0.913)
  Pallas kernels: 40.6 us -> 36.5 us
    pallas_call x1, Pallas kernels: 40.6 us -> 36.5 us  [shards(): pl.pallas_call(kernel_body, out_shape=(jax.ShapeDtypeStruct((8, 8, 32, 12...]
where the time goes in v1:
time: 43.1 us; the launch traced here: 42.9 us
  Pallas kernels  36.5 us (85%)
  local copies, waits for them, and re-layouts  5.73 us (13%)
  between operations  0.65 us (2%)
    pallas_call x1, Pallas kernels, shards(): pl.pallas_call(kernel_body, out_shape=(jax.ShapeDtypeStruct((8, 8, 32, 12...  36.5 us
    unnamed x9, local copies, waits for them, and re-layouts  5.73 us

profile of v1, /device:TPU:1, one launch (start us, length us, event | category | flops | bytes accessed | tf_op | source)
XLA Modules:
  0.0 42.9 jit_solution(15694834824932831416)
XLA Ops:
  0.6 0.0 copy-start
  0.6 1.0 %copy-done = bf16[8,8,32,128]{3,2,1,0:T(8,128)(2,1)S(1)} copy-done((bf16[8,8,32,128]{3,2,1,0:T(8,128)(2,1)S(1)}, bf16[8,8,32,128]{3,2,1,0:T(8,128)(2,1)}, u32[]{:S(2)}) %copy-start) | copy-done | bytes 524312
  1.7 0.0 copy-start.1
  1.7 1.0 %copy-done.1 = bf16[3,3,3,64,128]{4,3,2,1,0:T(8,128)(2,1)S(1)} copy-done((bf16[3,3,3,64,128]{4,3,2,1,0:T(8,128)(2,1)S(1)}, bf16[3,3,3,64,128]{4,3,2,1,0:T(8,128)(2,1)}, u32[]{:S(2)}) %copy-start.1) | copy-done | bytes 442392
  2.7 0.0 copy-start.2
  2.7 0.7 %copy-done.2 = s32[1,1,4]{2,1,0:T(1,128)S(1)} copy-done((s32[1,1,4]{2,1,0:T(1,128)S(1)}, s32[1,1,4]{2,1,0:T(1,128)}, u32[]{:S(2)}) %copy-start.2) | copy-done | bytes 40
  3.3 36.5 %shard_map.67 = (bf16[8,8,32,128]{3,2,1,0:T(8,128)(2,1)S(1)}, bf16[16,16,32,128]{3,2,1,0:T(8,128)(2,1)S(1)}, f32[1728,128]{1,0:T(8,128)S(1)}) custom-call(bf16[16,16,32,128]{3,2,1,0:T(8,128)(2,1)} %feat.1, s32[1,1,4]{2,1,0:T(1,128)S(1)} %copy-done.2, bf16[3,3,3,64,128]{4,3,2,1,0:T(8,128)(2,1)S(1)} %copy-done.1, bf16[8,8,32,128]{3,2,1,0:T(8,128)(2,1)S(1)} %copy-done), custom_call_target="tpu_custom_call" | custom-call | tf_op jit(solution)/shard_map/pallas_call | solution.py:299
  39.8 0.8 %copy.10 = bf16[8,8,32,128]{3,2,1,0:T(8,128)(2,1)} copy(bf16[8,8,32,128]{3,2,1,0:T(8,128)(2,1)S(1)} %get-tuple-element.12) | data formatting | bytes 1048576
  40.6 1.3 %copy.11 = bf16[16,16,32,128]{3,2,1,0:T(8,128)(2,1)} copy(bf16[16,16,32,128]{3,2,1,0:T(8,128)(2,1)S(1)} %get-tuple-element.13) | data formatting | bytes 4194304
  42.0 0.9 %copy.12 = f32[3,3,3,64,128]{4,3,2,1,0:T(8,128)} copy(f32[3,3,3,64,128]{4,3,2,1,0:T(8,128)S(1)} %bitcast.1) | data formatting | bytes 1769472
Async XLA Ops:
  0.6 1.0 %copy-start = (bf16[8,8,32,128]{3,2,1,0:T(8,128)(2,1)S(1)}, bf16[8,8,32,128]{3,2,1,0:T(8,128)(2,1)}, u32[]{:S(2)}) copy-start(bf16[8,8,32,128]{3,2,1,0:T(8,128)(2,1)} %ups.1) | copy-start | bytes 1572868
  1.7 1.0 %copy-start.1 = (bf16[3,3,3,64,128]{4,3,2,1,0:T(8,128)(2,1)S(1)}, bf16[3,3,3,64,128]{4,3,2,1,0:T(8,128)(2,1)}, u32[]{:S(2)}) copy-start(bf16[3,3,3,64,128]{4,3,2,1,0:T(8,128)(2,1)} %ker.1) | copy-start | bytes 1327108
  2.7 0.7 %copy-start.2 = (s32[1,1,4]{2,1,0:T(1,128)S(1)}, s32[1,1,4]{2,1,0:T(1,128)}, u32[]{:S(2)}) copy-start(s32[1,1,4]{2,1,0:T(1,128)} %occ.1) | copy-start | bytes 52

commit v2 on v1

--- a/solution.py
+++ b/solution.py
@@ -22,11 +22,11 @@
     return jnp.where(t == 0, 2, jnp.where(t == 1, 1, jnp.where(t == 2, 3, 0)))
 
 
-def peer(k, sign):
+def peer(k):
     x, y, z, c = coordinates()
-    px = (x + sign * far_first(k // 16) + 4) % 4
-    py = (y + sign * far_first((k // 4) % 4) + 4) % 4
-    pz = (z + sign * far_first(k % 4) + 4) % 4
+    px = (x + far_first(k >> 4)) & 3
+    py = (y + far_first((k >> 2) & 3)) & 3
+    pz = (z + far_first(k & 3)) & 3
     return px * 16 + py * 4 + pz, ((px * 4 + pz) * 2 + c, py)
 
 
@@ -41,10 +41,10 @@
 
 
 def kernel_body(
-    feat, occ, ker, ups, coarse, fgrad, kgrad,
+    feat, occ_h, ker, ups, coarse, fgrad, ag, ag_x,
     fv, gp, wv, mask, wide, gwt, wf, wd, acc,
     fz_s, fy_s, fz_r, fy_r, fc_r, gz_r, gy_r, gc_r,
-    pair_r, rs_r, ag, ag_x, co_v, fg_v, kg_v,
+    pair_r, rs_r, co_v, fg_v, occ, gwz, rim_z,
     gwy, rim_y, know, in_sem, hs_sem, hr_sem, pair_sem, rs_sem, ag_sem, out_sem,
 ):
     gz, gy = lax.axis_index("gz"), lax.axis_index("gy")
@@ -58,6 +58,7 @@
         pltpu.make_async_copy(ups, gp.at[0:8, 0:8], in_sem.at[0]),
         pltpu.make_async_copy(feat, fv, in_sem.at[1]),
         pltpu.make_async_copy(ker, wv, in_sem.at[2]),
+        pltpu.make_async_copy(occ_h, occ, in_sem.at[3]),
     ]
     for copy in copies:
         copy.start()
@@ -72,6 +73,7 @@
 
     pair = lax.broadcasted_iota(jnp.int32, (256, 128), 0) % 32
     held = jnp.zeros((256, 128), jnp.int32)
+    copies[3].wait()
     for k in range(4):
         held = jnp.where(pair // 8 == k, occ[0, 0, k], held)
     mask[...] = held.astype(F32)
@@ -88,25 +90,22 @@
     fz_s[...] = fv[15] * m32[None]
     fy_s[...] = fv[:, 15] * m32[None]
 
-    pl.semaphore_wait(barrier, 13)
-
-    halos = [
-        remote(fz_s, fz_r, hs_sem.at[0], hr_sem.at[0], (up, gy)),
-        remote(fy_s, fy_r, hs_sem.at[1], hr_sem.at[1], (gz, nxt)),
-        remote(fz_s.at[15], fc_r, hs_sem.at[2], hr_sem.at[2], (up, nxt)),
-        remote(gp.at[0, 0:8], gz_r, hs_sem.at[3], hr_sem.at[3], (down, gy)),
-        remote(gp.at[0:8, 0], gy_r, hs_sem.at[4], hr_sem.at[4], (gz, prv)),
-        remote(gp.at[0, 0], gc_r, hs_sem.at[5], hr_sem.at[5], (down, prv)),
-    ]
-    for copy in halos:
-        copy.start()
-    for device in along_y:
-        pl.semaphore_signal(know.at[0], inc=1, device_id=device, device_id_type=MESH)
+    copies[2].wait()
+    for tap in range(9):
+        kz, ky = tap // 3, tap % 3
+        rows = slice(tap * 128, tap * 128 + 128)
+        left = jnp.concatenate([wv[kz, ky, 1], wv[kz, ky, 2]], 0)
+        right = jnp.concatenate([jnp.zeros((64, 128), BF16), wv[kz, ky, 0]], 0)
+        wf[rows, 0:128] = left
+        wf[rows, 128:256] = right
+        wd[rows, 0:128] = left.astype(F32).T.astype(BF16)
+        wd[rows, 128:256] = right.astype(F32).T.astype(BF16)
 
     def turn(rows, ref, first):
-        flat = rows.reshape(256, 128).astype(F32)
-        later = jnp.where(pair == 31, 0.0, pltpu.roll(flat, 255, 0))
-        lanes = pl.ds(first if isinstance(first, int) else pl.multiple_of(first, 256), 256)
+        flat = rows.reshape(-1, 128).astype(F32)
+        count = flat.shape[0]
+        later = jnp.where(pair[:count] == 31, 0.0, pltpu.roll(flat, count - 1, 0))
+        lanes = pl.ds(first if isinstance(first, int) else pl.multiple_of(first, 256), count)
         ref[0:128, lanes] = flat.T.astype(BF16)
         ref[128:256, lanes] = later.T.astype(BF16)
 
@@ -115,7 +114,16 @@
         return 0
 
     lax.fori_loop(0, 8, turn_plane, 0)
-    turn(gp[0:8, 0], gwy, 0)
+    for ky in range(3):
+        for b in range(12):
+            row = 2 * b - 1 + ky
+            edge = fz_s[row] if 0 <= row < 16 else jnp.zeros((32, 128), BF16)
+            rim_z[b * 32 : b * 32 + 32, ky * 128 : ky * 128 + 128] = edge
+    for kz in range(3):
+        for a in range(8):
+            plane = 2 * a - 1 + kz
+            edge = fy_s[plane] if plane >= 0 else jnp.zeros((32, 128), BF16)
+            rim_y[a * 32 : a * 32 + 32, kz * 128 : kz * 128 + 128] = edge
 
     def widen(a, first):
         for kz in range(3):
@@ -147,33 +155,46 @@
             acc[tap * 192 + 64 : tap * 192 + 192] = piece[:128].T
             acc[tap * 192 : tap * 192 + 64] = piece[128:].T[64:]
 
+    pl.semaphore_wait(barrier, 13)
+
+    halos = [
+        remote(gp.at[0, 0], gc_r, hs_sem.at[0], hr_sem.at[0], (down, prv)),
+        remote(gp.at[0:8, 0], gy_r, hs_sem.at[1], hr_sem.at[1], (gz, prv)),
+        remote(gp.at[0, 0:8], gz_r, hs_sem.at[2], hr_sem.at[2], (down, gy)),
+        remote(fy_s, fy_r, hs_sem.at[3], hr_sem.at[3], (gz, nxt)),
+        remote(fz_s, fz_r, hs_sem.at[4], hr_sem.at[4], (up, gy)),
+        remote(fz_s.at[15], fc_r, hs_sem.at[5], hr_sem.at[5], (up, nxt)),
+    ]
+    for copy in halos[:3]:
+        copy.start()
+    for device in along_y:
+        pl.semaphore_signal(know.at[0], inc=1, device_id=device, device_id_type=MESH)
+    for copy in halos[3:]:
+        copy.start()
+
     pl.semaphore_wait(know.at[0], 3)
     for device in along_x:
         pl.semaphore_signal(know.at[1], inc=1, device_id=device, device_id_type=MESH)
 
     for copy in halos[:3]:
         copy.wait_recv()
-
-    has_z = jnp.where(gz > 0, 1.0, 0.0) * jnp.ones((32, 128), F32)
-    has_y = jnp.where(gy > 0, 1.0, 0.0) * jnp.ones((32, 128), F32)
-    z_on, y_on, c_on = has_z.astype(BF16), has_y.astype(BF16), (has_z * has_y).astype(BF16)
-    for ky in range(3):
-        for b in range(8):
-            row = 2 * b - 1 + ky
-            rim = fc_r[...] * c_on if row < 0 else fz_r[row] * z_on
-            wide[b * 32 : b * 32 + 32, ky * 128 : ky * 128 + 128] = rim
-    for a in range(8):
-        for kz in range(3):
-            plane = 2 * a - 1 + kz
-            rim = fy_r[plane] * y_on if plane >= 0 else jnp.zeros((32, 128), BF16)
-            rim_y[a * 32 : a * 32 + 32, kz * 128 : kz * 128 + 128] = rim
-            if plane >= 0:
-                wide[a * 256 : a * 256 + 32, kz * 384 : kz * 384 + 128] = rim
-    by_z = jnp.dot(gwt[:, 0:256], wide[0:256, 0:384], preferred_element_type=F32)
+    last_z = jnp.where(gz < 31, 1.0, 0.0) * jnp.ones((32, 128), F32)
+    last_y = jnp.where(gy < 3, 1.0, 0.0) * jnp.ones((32, 128), F32)
+    gp[8, 0:8] = gz_r[...] * last_z.astype(BF16)[None]
+    gp[0:8, 8] = gy_r[...] * last_y.astype(BF16)[None]
+    gp[8, 8] = gc_r[...] * (last_z * last_y).astype(BF16)
+    turn(gp[8, 0:8], gwz, 0)
+    turn(jnp.concatenate([gp[8, 8], jnp.zeros((96, 128), BF16)], 0), gwz, 256)
+    turn(gp[0:8, 8], gwy, 0)
+    by_z = jnp.dot(gwz[...], rim_z[...], preferred_element_type=F32)
     by_y = jnp.dot(gwy[...], rim_y[...], preferred_element_type=F32)
-    for tap, terms in ((0, by_z), (1, by_z), (2, by_z), (0, by_y), (3, by_y), (6, by_y)):
-        at = tap if terms is by_z else tap // 3
-        piece = terms[:, at * 128 : at * 128 + 128]
+    for tap in (0, 1, 2, 3, 6):
+        if tap == 0:
+            piece = by_z[:, 0:128] + by_y[:, 0:128]
+        elif tap < 3:
+            piece = by_z[:, tap * 128 : tap * 128 + 128]
+        else:
+            piece = by_y[:, tap // 3 * 128 : tap // 3 * 128 + 128]
         acc[tap * 192 + 64 : tap * 192 + 192] += piece[:128].T
         acc[tap * 192 : tap * 192 + 64] += piece[128:].T[64:]
 
@@ -187,33 +208,12 @@
     pl.semaphore_wait(know.at[1], 3)
 
     def scatter(k, _):
-        j, device = peer(k, 1)
+        j, device = peer(k)
         row = pl.multiple_of(c * HALF + chunk_row(j), 8)
         remote(acc.at[pl.ds(row, CHUNK)], rs_r.at[k], rs_sem.at[0], rs_sem.at[1], device).start()
         return 0
 
     lax.fori_loop(0, PEERS, scatter, 0)
-
-    copies[2].wait()
-    for tap in range(9):
-        kz, ky = tap // 3, tap % 3
-        rows = slice(tap * 128, tap * 128 + 128)
-        left = jnp.concatenate([wv[kz, ky, 1], wv[kz, ky, 2]], 0)
-        right = jnp.concatenate([jnp.zeros((64, 128), BF16), wv[kz, ky, 0]], 0)
-        wf[rows, 0:128] = left
-        wf[rows, 128:256] = right
-        wd[rows, 0:128] = left.astype(F32).T.astype(BF16)
-        wd[rows, 128:256] = right.astype(F32).T.astype(BF16)
-
-    for copy in halos[3:]:
-        copy.wait_recv()
-    for copy in halos:
-        copy.wait_send()
-    last_z = (jnp.where(gz < 31, 1.0, 0.0) * jnp.ones((32, 128), F32))
-    last_y = (jnp.where(gy < 3, 1.0, 0.0) * jnp.ones((32, 128), F32))
-    gp[8, 0:8] = gz_r[...] * last_z.astype(BF16)[None]
-    gp[0:8, 8] = gy_r[...] * last_y.astype(BF16)[None]
-    gp[8, 8] = gc_r[...] * (last_z * last_y).astype(BF16)
 
     def tap_rows(kz, ky):
         return wd[(kz * 3 + ky) * 128 : (kz * 3 + ky) * 128 + 128]
@@ -242,13 +242,31 @@
     fg_out = pltpu.make_async_copy(fg_v, fgrad, out_sem.at[0])
     fg_out.start()
 
+    for copy in halos[3:]:
+        copy.wait_recv()
+    for copy in halos:
+        copy.wait_send()
+    has_z = jnp.where(gz > 0, 1.0, 0.0) * jnp.ones((32, 128), F32)
+    has_y = jnp.where(gy > 0, 1.0, 0.0) * jnp.ones((32, 128), F32)
+    z_on, y_on, c_on = has_z.astype(BF16), has_y.astype(BF16), (has_z * has_y).astype(BF16)
+    for ky in range(3):
+        for b in range(8):
+            row = 2 * b - 1 + ky
+            rim = fc_r[...] * c_on if row < 0 else fz_r[row] * z_on
+            wide[b * 32 : b * 32 + 32, ky * 128 : ky * 128 + 128] = rim
+    for a in range(8):
+        for kz in range(3):
+            plane = 2 * a - 1 + kz
+            if plane >= 0:
+                wide[a * 256 : a * 256 + 32, kz * 384 : kz * 384 + 128] = fy_r[plane] * y_on
+
     pltpu.make_async_copy(rs_r, rs_r, rs_sem.at[1]).wait()
     own = acc[pl.ds(pl.multiple_of(c * HALF + chunk_row(me), 8), CHUNK)]
     total = lax.fori_loop(0, PEERS, lambda k, t: t + rs_r[k], own)
     ag[me] = total.astype(BF16)
 
     def gather(k, _):
-        remote(ag.at[me], ag.at[me], ag_sem.at[0], ag_sem.at[1], peer(k, 1)[1]).start()
+        remote(ag.at[me], ag.at[me], ag_sem.at[0], ag_sem.at[1], peer(k)[1]).start()
         return 0
 
     lax.fori_loop(0, PEERS, gather, 0)
@@ -268,43 +286,51 @@
     trade = remote(ag, ag_x, pair_sem.at[2], pair_sem.at[3], other)
     trade.start()
 
-    def place(buffer, base):
-        def put(j, _):
-            row = pl.multiple_of(base + chunk_row(j), 8)
-            kg_v[pl.ds(row, CHUNK)] = buffer[j].astype(F32)
-            return 0
-
-        lax.fori_loop(0, 64, put, 0)
-
-    place(ag, mine)
     trade.wait_recv()
-    place(ag_x, theirs)
-    kg_out = pltpu.make_async_copy(kg_v, kgrad, out_sem.at[2])
-    kg_out.start()
-
     swap.wait_send()
     trade.wait_send()
     pltpu.make_async_copy(rs_r, rs_r, rs_sem.at[0]).wait()
     pltpu.make_async_copy(ag.at[0:PEERS], ag.at[0:PEERS], ag_sem.at[0]).wait()
     fg_out.wait()
     co_out.wait()
-    kg_out.wait()
+
+
+def finish_body(coarse, fgrad, ag, ag_x, coarse_out, fgrad_out, kgrad_out, kg_v, sem):
+    first = pltpu.make_async_copy(fgrad, fgrad_out, sem.at[0])
+    second = pltpu.make_async_copy(coarse, coarse_out, sem.at[1])
+    first.start()
+    second.start()
+    c = lax.axis_index("gz") & 1
+    for buffer, half in ((ag, c), (ag_x, 1 - c)):
+        for j in range(64):
+            row = pl.multiple_of(half * HALF + chunk_row(j), 8)
+            kg_v[pl.ds(row, CHUNK)] = buffer[j].astype(F32)
+    third = pltpu.make_async_copy(kg_v, kgrad_out, sem.at[2])
+    third.start()
+    first.wait()
+    second.wait()
+    third.wait()
 
 
 def shards(features, occupancy, kernel, upstream):
     vm = pltpu.VMEM
     dma = pltpu.SemaphoreType.DMA
     any_space = pl.BlockSpec(memory_space=pl.ANY)
-    hbm = pl.BlockSpec(memory_space=pltpu.HBM)
-    coarse, fgrad, kgrad = pl.pallas_call(
+    in_vmem = pl.BlockSpec(memory_space=pltpu.VMEM)
+    shapes = (
+        jax.ShapeDtypeStruct((8, 8, 32, 128), BF16),
+        jax.ShapeDtypeStruct((16, 16, 32, 128), BF16),
+    )
+    gathered = jax.ShapeDtypeStruct((64, CHUNK, 128), BF16)
+    arguments = [
+        pltpu.with_memory_space_constraint(a, pltpu.HBM)
+        for a in (features, occupancy, kernel, upstream)
+    ]
+    parts = pl.pallas_call(
         kernel_body,
-        out_shape=(
-            jax.ShapeDtypeStruct((8, 8, 32, 128), BF16),
-            jax.ShapeDtypeStruct((16, 16, 32, 128), BF16),
-            jax.ShapeDtypeStruct((1728, 128), F32),
-        ),
-        in_specs=[hbm, pl.BlockSpec(memory_space=pltpu.SMEM), hbm, hbm],
-        out_specs=(any_space, any_space, any_space),
+        out_shape=shapes + (gathered, gathered),
+        in_specs=[any_space] * 4,
+        out_specs=(any_space, any_space, in_vmem, in_vmem),
         scratch_shapes=[
             vm((16, 16, 32, 128), BF16),
             vm((9, 9, 32, 128), BF16),
@@ -325,26 +351,34 @@
             vm((32, 128), BF16),
             vm((HALF, 128), F32),
             vm((PEERS, CHUNK, 128), F32),
-            vm((64, CHUNK, 128), BF16),
-            vm((64, CHUNK, 128), BF16),
             vm((8, 8, 32, 128), BF16),
             vm((16, 16, 32, 128), BF16),
-            vm((1728, 128), F32),
+            pltpu.SMEM((1, 1, 4), jnp.int32),
+            vm((256, 384), BF16),
+            vm((384, 384), BF16),
             vm((256, 256), BF16),
             vm((256, 384), BF16),
             pltpu.SemaphoreType.REGULAR((2,)),
-            dma((3,)),
+            dma((4,)),
             dma((6,)),
             dma((6,)),
             dma((4,)),
             dma((2,)),
             dma((2,)),
-            dma((3,)),
+            dma((2,)),
         ],
         compiler_params=pltpu.CompilerParams(
             collective_id=0, has_side_effects=True, vmem_limit_bytes=48 * 1024 * 1024
         ),
-    )(features, occupancy, kernel, upstream)
+    )(*arguments)
+    coarse, fgrad, kgrad = pl.pallas_call(
+        finish_body,
+        out_shape=shapes + (jax.ShapeDtypeStruct((1728, 128), F32),),
+        in_specs=[any_space, any_space, in_vmem, in_vmem],
+        out_specs=(any_space,) * 3,
+        scratch_shapes=[vm((1728, 128), F32), dma((3,))],
+        compiler_params=pltpu.CompilerParams(vmem_limit_bytes=4 * 1024 * 1024),
+    )(*parts)
     return coarse, fgrad, kgrad.reshape(3, 3, 3, 64, 128)
 
 

time: 43.1 us -> 37.6 us (0.87)
  local copies, waits for them, and re-layouts: 5.73 us -> 0 us
    unnamed x9 -> x0, local copies, waits for them, and re-layouts: 5.73 us -> none
    pallas_call x1 -> x2, Pallas kernels: 36.5 us -> 36.8 us  [the longest x1 35 us: shards(): pl.pallas_call(kernel_body, out_shape=shapes + (gathered, gathered), in_s...]
where the time goes in v2:
time: 37.6 us; the launch traced here: 37.4 us
  Pallas kernels  36.8 us (98%)
  between operations  0.64 us (2%)
    pallas_call x1, Pallas kernels, shards(): pl.pallas_call(kernel_body, out_shape=shapes + (gathered, gathered), in_s...  35 us
    pallas_call x1, Pallas kernels, shards(): pl.pallas_call(finish_body, out_shape=shapes + (jax.ShapeDtypeStruct((172...  1.8 us

profile of v2, /device:TPU:1, one launch (start us, length us, event | category | flops | bytes accessed | tf_op | source)
XLA Modules:
  0.0 37.4 jit_solution(1378255018012018774)
XLA Ops:
  0.6 35.0 %shard_map.67 = (bf16[8,8,32,128]{3,2,1,0:T(8,128)(2,1)S(1)}, bf16[16,16,32,128]{3,2,1,0:T(8,128)(2,1)S(1)}, bf16[64,16,128]{2,1,0:T(8,128)(2,1)S(1)}, bf16[64,16,128]{2,1,0:T(8,128)(2,1)S(1)}) custom-call(bf16[16,16,32,128]{3,2,1,0:T(8,128)(2,1)} %feat.1, s32[1,1,4]{2,1,0:T(1,128)} %occ_h.1, bf16[3,3,3,64,128]{4,3,2,1,0:T(8,128)(2,1)} %ker.1, ...), custom_call_target="tpu_custom_call" | custom-call | tf_op jit(solution)/shard_map/pallas_call | solution.py:329
  35.6 1.8 %shard_map.68 = (bf16[8,8,32,128]{3,2,1,0:T(8,128)(2,1)}, bf16[16,16,32,128]{3,2,1,0:T(8,128)(2,1)}, f32[1728,128]{1,0:T(8,128)}) custom-call(bf16[8,8,32,128]{3,2,1,0:T(8,128)(2,1)S(1)} %get-tuple-element.10.coarse, bf16[16,16,32,128]{3,2,1,0:T(8,128)(2,1)S(1)} %get-tuple-element.11.fgrad, bf16[64,16,128]{2,1,0:T(8,128)(2,1)S(1)} %get-tuple-element.12.ag, ...), custom_call_target="tpu_custom_call" | custom-call | tf_op jit(solution)/shard_map/pallas_call | solution.py:374

commit v3 on v2

--- a/solution.py
+++ b/solution.py
@@ -10,6 +10,7 @@
 BF16 = jnp.bfloat16
 HALF = 864
 CHUNK = 16
+OWNERS = 54
 PEERS = 63
 
 
@@ -28,10 +29,6 @@
     py = (y + far_first((k >> 2) & 3)) & 3
     pz = (z + far_first(k & 3)) & 3
     return px * 16 + py * 4 + pz, ((px * 4 + pz) * 2 + c, py)
-
-
-def chunk_row(j):
-    return ((j * 106) // 63) * 8
 
 
 def remote(src, dst, send, recv, device):
@@ -86,75 +83,6 @@
         return 0
 
     lax.fori_loop(0, 8, mask_grad, 0)
-    copies[1].wait()
-    fz_s[...] = fv[15] * m32[None]
-    fy_s[...] = fv[:, 15] * m32[None]
-
-    copies[2].wait()
-    for tap in range(9):
-        kz, ky = tap // 3, tap % 3
-        rows = slice(tap * 128, tap * 128 + 128)
-        left = jnp.concatenate([wv[kz, ky, 1], wv[kz, ky, 2]], 0)
-        right = jnp.concatenate([jnp.zeros((64, 128), BF16), wv[kz, ky, 0]], 0)
-        wf[rows, 0:128] = left
-        wf[rows, 128:256] = right
-        wd[rows, 0:128] = left.astype(F32).T.astype(BF16)
-        wd[rows, 128:256] = right.astype(F32).T.astype(BF16)
-
-    def turn(rows, ref, first):
-        flat = rows.reshape(-1, 128).astype(F32)
-        count = flat.shape[0]
-        later = jnp.where(pair[:count] == 31, 0.0, pltpu.roll(flat, count - 1, 0))
-        lanes = pl.ds(first if isinstance(first, int) else pl.multiple_of(first, 256), count)
-        ref[0:128, lanes] = flat.T.astype(BF16)
-        ref[128:256, lanes] = later.T.astype(BF16)
-
-    def turn_plane(a, _):
-        turn(gp[a, 0:8], gwt, a * 256)
-        return 0
-
-    lax.fori_loop(0, 8, turn_plane, 0)
-    for ky in range(3):
-        for b in range(12):
-            row = 2 * b - 1 + ky
-            edge = fz_s[row] if 0 <= row < 16 else jnp.zeros((32, 128), BF16)
-            rim_z[b * 32 : b * 32 + 32, ky * 128 : ky * 128 + 128] = edge
-    for kz in range(3):
-        for a in range(8):
-            plane = 2 * a - 1 + kz
-            edge = fy_s[plane] if plane >= 0 else jnp.zeros((32, 128), BF16)
-            rim_y[a * 32 : a * 32 + 32, kz * 128 : kz * 128 + 128] = edge
-
-    def widen(a, first):
-        for kz in range(3):
-            for ky in range(3):
-                tap = kz * 3 + ky
-                for b in range(8):
-                    rows = pl.ds(pl.multiple_of(a * 256 + b * 32, 32), 32)
-                    if (first and kz == 0) or (ky == 0 and b == 0):
-                        piece = jnp.zeros((32, 128), BF16)
-                    else:
-                        piece = fv[2 * a - 1 + kz, 2 * b - 1 + ky] * m32
-                    wide[rows, tap * 128 : tap * 128 + 128] = piece
-
-    widen(0, True)
-
-    def widen_later(a, _):
-        widen(a, False)
-        return 0
-
-    lax.fori_loop(1, 8, widen_later, 0)
-
-    for first in range(0, 9, 2):
-        taps = range(first, min(first + 2, 9))
-        out = jnp.dot(
-            gwt[...], wide[:, first * 128 : (taps[-1] + 1) * 128], preferred_element_type=F32
-        )
-        for tap in taps:
-            piece = out[:, (tap - first) * 128 : (tap - first) * 128 + 128]
-            acc[tap * 192 + 64 : tap * 192 + 192] = piece[:128].T
-            acc[tap * 192 : tap * 192 + 64] = piece[128:].T[64:]
-
     pl.semaphore_wait(barrier, 13)
 
     halos = [
@@ -169,8 +97,76 @@
         copy.start()
     for device in along_y:
         pl.semaphore_signal(know.at[0], inc=1, device_id=device, device_id_type=MESH)
+    copies[1].wait()
+    fz_s[...] = fv[15] * m32[None]
+    fy_s[...] = fv[:, 15] * m32[None]
     for copy in halos[3:]:
         copy.start()
+
+    copies[2].wait()
+    for tap in range(9):
+        kz, ky = tap // 3, tap % 3
+        rows = slice(tap * 128, tap * 128 + 128)
+        left = jnp.concatenate([wv[kz, ky, 1], wv[kz, ky, 2]], 0)
+        right = jnp.concatenate([jnp.zeros((64, 128), BF16), wv[kz, ky, 0]], 0)
+        wf[rows, 0:128] = left
+        wf[rows, 128:256] = right
+        wd[rows, 0:128] = left.astype(F32).T.astype(BF16)
+        wd[rows, 128:256] = right.astype(F32).T.astype(BF16)
+
+    def turn(rows, ref, first):
+        flat = rows.reshape(-1, 128).astype(F32)
+        count = flat.shape[0]
+        later = jnp.where(pair[:count] == 31, 0.0, pltpu.roll(flat, count - 1, 0))
+        lanes = pl.ds(first if isinstance(first, int) else pl.multiple_of(first, 256), count)
+        ref[0:128, lanes] = flat.T.astype(BF16)
+        ref[128:256, lanes] = later.T.astype(BF16)
+
+    def turn_plane(a, _):
+        turn(gp[a, 0:8], gwt, a * 256)
+        return 0
+
+    lax.fori_loop(0, 8, turn_plane, 0)
+    for ky in range(3):
+        for b in range(12):
+            row = 2 * b - 1 + ky
+            edge = fz_s[row] if 0 <= row < 16 else jnp.zeros((32, 128), BF16)
+            rim_z[b * 32 : b * 32 + 32, ky * 128 : ky * 128 + 128] = edge
+    for kz in range(3):
+        for a in range(8):
+            plane = 2 * a - 1 + kz
+            edge = fy_s[plane] if plane >= 0 else jnp.zeros((32, 128), BF16)
+            rim_y[a * 32 : a * 32 + 32, kz * 128 : kz * 128 + 128] = edge
+
+    def widen(a, first):
+        for kz in range(3):
+            for ky in range(3):
+                tap = kz * 3 + ky
+                for b in range(8):
+                    rows = pl.ds(pl.multiple_of(a * 256 + b * 32, 32), 32)
+                    if (first and kz == 0) or (ky == 0 and b == 0):
+                        piece = jnp.zeros((32, 128), BF16)
+                    else:
+                        piece = fv[2 * a - 1 + kz, 2 * b - 1 + ky] * m32
+                    wide[rows, tap * 128 : tap * 128 + 128] = piece
+
+    widen(0, True)
+
+    def widen_later(a, _):
+        widen(a, False)
+        return 0
+
+    lax.fori_loop(1, 8, widen_later, 0)
+
+    for first in range(0, 9, 2):
+        taps = range(first, min(first + 2, 9))
+        out = jnp.dot(
+            gwt[...], wide[:, first * 128 : (taps[-1] + 1) * 128], preferred_element_type=F32
+        )
+        for tap in taps:
+            piece = out[:, (tap - first) * 128 : (tap - first) * 128 + 128]
+            acc[tap * 192 + 64 : tap * 192 + 192] = piece[:128].T
+            acc[tap * 192 : tap * 192 + 64] = piece[128:].T[64:]
 
     pl.semaphore_wait(know.at[0], 3)
     for device in along_x:
@@ -209,8 +205,12 @@
 
     def scatter(k, _):
         j, device = peer(k)
-        row = pl.multiple_of(c * HALF + chunk_row(j), 8)
-        remote(acc.at[pl.ds(row, CHUNK)], rs_r.at[k], rs_sem.at[0], rs_sem.at[1], device).start()
+
+        @pl.when(j < OWNERS)
+        def _():
+            row = pl.multiple_of(mine + j * CHUNK, CHUNK)
+            remote(acc.at[pl.ds(row, CHUNK)], rs_r.at[k], rs_sem.at[0], rs_sem.at[1], device).start()
+
         return 0
 
     lax.fori_loop(0, PEERS, scatter, 0)
@@ -260,16 +260,16 @@
             if plane >= 0:
                 wide[a * 256 : a * 256 + 32, kz * 384 : kz * 384 + 128] = fy_r[plane] * y_on
 
-    pltpu.make_async_copy(rs_r, rs_r, rs_sem.at[1]).wait()
-    own = acc[pl.ds(pl.multiple_of(c * HALF + chunk_row(me), 8), CHUNK)]
-    total = lax.fori_loop(0, PEERS, lambda k, t: t + rs_r[k], own)
-    ag[me] = total.astype(BF16)
-
     def gather(k, _):
         remote(ag.at[me], ag.at[me], ag_sem.at[0], ag_sem.at[1], peer(k)[1]).start()
         return 0
 
-    lax.fori_loop(0, PEERS, gather, 0)
+    @pl.when(me < OWNERS)
+    def _():
+        pltpu.make_async_copy(rs_r, rs_r, rs_sem.at[1]).wait()
+        own = acc[pl.ds(pl.multiple_of(mine + me * CHUNK, CHUNK), CHUNK)]
+        ag[me] = (own + jnp.sum(rs_r[...], 0)).astype(BF16)
+        lax.fori_loop(0, PEERS, gather, 0)
 
     def forward(a, _):
         rows = pl.ds(pl.multiple_of(a * 256, 256), 256)
@@ -282,15 +282,33 @@
     co_out = pltpu.make_async_copy(co_v, coarse, out_sem.at[1])
     co_out.start()
 
-    pltpu.make_async_copy(ag.at[0:PEERS], ag.at[0:PEERS], ag_sem.at[1]).wait()
+    @pl.when(me < OWNERS)
+    def _():
+        pltpu.make_async_copy(ag.at[1:OWNERS], ag.at[1:OWNERS], ag_sem.at[1]).wait()
+
+    @pl.when(me >= OWNERS)
+    def _():
+        pltpu.make_async_copy(ag, ag, ag_sem.at[1]).wait()
+
     trade = remote(ag, ag_x, pair_sem.at[2], pair_sem.at[3], other)
     trade.start()
 
     trade.wait_recv()
     swap.wait_send()
     trade.wait_send()
-    pltpu.make_async_copy(rs_r, rs_r, rs_sem.at[0]).wait()
-    pltpu.make_async_copy(ag.at[0:PEERS], ag.at[0:PEERS], ag_sem.at[0]).wait()
+
+    @pl.when(me < OWNERS)
+    def _():
+        sent = rs_r.at[1:OWNERS]
+        pltpu.make_async_copy(sent, sent, rs_sem.at[0]).wait()
+        for part in (ag, ag.at[1 : PEERS - OWNERS + 1]):
+            pltpu.make_async_copy(part, part, ag_sem.at[0]).wait()
+
+    @pl.when(me >= OWNERS)
+    def _():
+        sent = rs_r.at[0:OWNERS]
+        pltpu.make_async_copy(sent, sent, rs_sem.at[0]).wait()
+
     fg_out.wait()
     co_out.wait()
 
@@ -302,8 +320,8 @@
     second.start()
     c = lax.axis_index("gz") & 1
     for buffer, half in ((ag, c), (ag_x, 1 - c)):
-        for j in range(64):
-            row = pl.multiple_of(half * HALF + chunk_row(j), 8)
+        for j in range(OWNERS):
+            row = pl.multiple_of(half * HALF + j * CHUNK, CHUNK)
             kg_v[pl.ds(row, CHUNK)] = buffer[j].astype(F32)
     third = pltpu.make_async_copy(kg_v, kgrad_out, sem.at[2])
     third.start()
@@ -321,7 +339,7 @@
         jax.ShapeDtypeStruct((8, 8, 32, 128), BF16),
         jax.ShapeDtypeStruct((16, 16, 32, 128), BF16),
     )
-    gathered = jax.ShapeDtypeStruct((64, CHUNK, 128), BF16)
+    gathered = jax.ShapeDtypeStruct((OWNERS, CHUNK, 128), BF16)
     arguments = [
         pltpu.with_memory_space_constraint(a, pltpu.HBM)
         for a in (features, occupancy, kernel, upstream)

time: 37.6 us -> 34.6 us (0.920)
  Pallas kernels: 36.8 us -> 33.8 us
    pallas_call x1, Pallas kernels: 35 us -> 32 us  [shards(): pl.pallas_call(kernel_body, out_shape=shapes + (gathered, gathered), in_s...]
where the time goes in v3:
time: 34.6 us; the launch traced here: 34.5 us
  Pallas kernels  33.8 us (98%)
  between operations  0.64 us (2%)
    pallas_call x1, Pallas kernels, shards(): pl.pallas_call(kernel_body, out_shape=shapes + (gathered, gathered), in_s...  32 us
    pallas_call x1, Pallas kernels, shards(): pl.pallas_call(finish_body, out_shape=shapes + (jax.ShapeDtypeStruct((172...  1.8 us

profile of v3, /device:TPU:1, one launch (start us, length us, event | category | flops | bytes accessed | tf_op | source)
XLA Modules:
  0.0 34.5 jit_solution(10746827763726843546)
XLA Ops:
  0.6 32.0 %shard_map.67 = (bf16[8,8,32,128]{3,2,1,0:T(8,128)(2,1)S(1)}, bf16[16,16,32,128]{3,2,1,0:T(8,128)(2,1)S(1)}, bf16[54,16,128]{2,1,0:T(8,128)(2,1)S(1)}, bf16[54,16,128]{2,1,0:T(8,128)(2,1)S(1)}) custom-call(bf16[16,16,32,128]{3,2,1,0:T(8,128)(2,1)} %feat.1, s32[1,1,4]{2,1,0:T(1,128)} %occ_h.1, bf16[3,3,3,64,128]{4,3,2,1,0:T(8,128)(2,1)} %ker.1, ...), custom_call_target="tpu_custom_call" | custom-call | tf_op jit(solution)/shard_map/pallas_call | solution.py:347
  32.7 1.8 %shard_map.68 = (bf16[8,8,32,128]{3,2,1,0:T(8,128)(2,1)}, bf16[16,16,32,128]{3,2,1,0:T(8,128)(2,1)}, f32[1728,128]{1,0:T(8,128)}) custom-call(bf16[8,8,32,128]{3,2,1,0:T(8,128)(2,1)S(1)} %get-tuple-element.10.coarse, bf16[16,16,32,128]{3,2,1,0:T(8,128)(2,1)S(1)} %get-tuple-element.11.fgrad, bf16[54,16,128]{2,1,0:T(8,128)(2,1)S(1)} %get-tuple-element.12.ag, ...), custom_call_target="tpu_custom_call" | custom-call | tf_op jit(solution)/shard_map/pallas_call | solution.py:392

commit v4 on v3

--- a/solution.py
+++ b/solution.py
@@ -9,6 +9,8 @@
 F32 = jnp.float32
 BF16 = jnp.bfloat16
 HALF = 864
+EARLY = 384
+LATE = 480
 CHUNK = 16
 OWNERS = 54
 PEERS = 63
@@ -16,19 +18,30 @@
 
 def coordinates():
     gz, gy = lax.axis_index("gz"), lax.axis_index("gy")
-    return gz // 8, gy, (gz // 2) % 4, gz % 2
-
-
-def far_first(t):
-    return jnp.where(t == 0, 2, jnp.where(t == 1, 1, jnp.where(t == 2, 3, 0)))
-
-
-def peer(k):
+    return gz >> 3, gy, (gz >> 1) & 3, gz & 1
+
+
+def hops(offset):
+    return sum(min(o, 4 - o) for o in offset)
+
+
+OFFSETS = sorted(
+    [(i, j, k) for i in range(4) for j in range(4) for k in range(4) if i + j + k], key=hops, reverse=True
+)
+
+
+def number(x, y, z):
+    return ((x * 16 + y * 4 + z) * 37) & 63
+
+
+def peer(offset):
     x, y, z, c = coordinates()
-    px = (x + far_first(k >> 4)) & 3
-    py = (y + far_first((k >> 2) & 3)) & 3
-    pz = (z + far_first(k & 3)) & 3
-    return px * 16 + py * 4 + pz, ((px * 4 + pz) * 2 + c, py)
+    px, py, pz = (x + offset[0]) & 3, (y + offset[1]) & 3, (z + offset[2]) & 3
+    return number(px, py, pz), ((px * 4 + pz) * 2 + c, py)
+
+
+def first_row(tap):
+    return (4, 5, 0, 1, 2, 3, 6, 7, 8).index(tap) * 192
 
 
 def remote(src, dst, send, recv, device):
@@ -38,18 +51,26 @@
 
 
 def kernel_body(
-    feat, occ_h, ker, ups, coarse, fgrad, ag, ag_x,
+    feat, occ_h, ker, ups, coarse, fgrad, kg,
     fv, gp, wv, mask, wide, gwt, wf, wd, acc,
     fz_s, fy_s, fz_r, fy_r, fc_r, gz_r, gy_r, gc_r,
-    pair_r, rs_r, co_v, fg_v, occ, gwz, rim_z,
+    pair_r, rs_r, ag, ag_x, co_v, fg_v, occ, gwz, rim_z,
     gwy, rim_y, know, in_sem, hs_sem, hr_sem, pair_sem, rs_sem, ag_sem, out_sem,
 ):
     gz, gy = lax.axis_index("gz"), lax.axis_index("gy")
     x, y, z, c = coordinates()
-    me = x * 16 + y * 4 + z
+    me = number(x, y, z)
     other = (gz + 1 - 2 * c, gy)
     up, down = (gz + 1) % 32, (gz + 31) % 32
     nxt, prv = (gy + 1) % 4, (gy + 3) % 4
+
+    barrier = pltpu.get_barrier_semaphore()
+    along_x = [((((x + i) % 4) * 4 + z) * 2 + c, gy) for i in (2, 1, 3)]
+    along_y = [(gz, (gy + i) % 4) for i in (2, 1, 3)]
+    along_z = [((x * 4 + (z + i) % 4) * 2 + c, gy) for i in (2, 1, 3)]
+    beside = [(up, nxt), (down, prv), (up, gy), (down, gy)]
+    for device in beside + along_y + along_x + along_z:
+        pl.semaphore_signal(barrier, inc=1, device_id=device, device_id_type=MESH)
 
     copies = [
         pltpu.make_async_copy(ups, gp.at[0:8, 0:8], in_sem.at[0]),
@@ -59,14 +80,6 @@
     ]
     for copy in copies:
         copy.start()
-
-    barrier = pltpu.get_barrier_semaphore()
-    along_x = [((((x + i) % 4) * 4 + z) * 2 + c, gy) for i in (2, 1, 3)]
-    along_y = [(gz, (gy + i) % 4) for i in (2, 1, 3)]
-    along_z = [((x * 4 + (z + i) % 4) * 2 + c, gy) for i in (2, 1, 3)]
-    beside = [(up, nxt), (down, prv), (up, gy), (down, gy)]
-    for device in beside + along_y + along_x + along_z:
-        pl.semaphore_signal(barrier, inc=1, device_id=device, device_id_type=MESH)
 
     pair = lax.broadcasted_iota(jnp.int32, (256, 128), 0) % 32
     held = jnp.zeros((256, 128), jnp.int32)
@@ -111,16 +124,16 @@
         right = jnp.concatenate([jnp.zeros((64, 128), BF16), wv[kz, ky, 0]], 0)
         wf[rows, 0:128] = left
         wf[rows, 128:256] = right
-        wd[rows, 0:128] = left.astype(F32).T.astype(BF16)
-        wd[rows, 128:256] = right.astype(F32).T.astype(BF16)
+        wd[rows, 0:128] = left.T
+        wd[rows, 128:256] = right.T
 
     def turn(rows, ref, first):
         flat = rows.reshape(-1, 128).astype(F32)
         count = flat.shape[0]
         later = jnp.where(pair[:count] == 31, 0.0, pltpu.roll(flat, count - 1, 0))
         lanes = pl.ds(first if isinstance(first, int) else pl.multiple_of(first, 256), count)
-        ref[0:128, lanes] = flat.T.astype(BF16)
-        ref[128:256, lanes] = later.T.astype(BF16)
+        ref[0:128, lanes] = rows.reshape(-1, 128).T
+        ref[128:256, lanes] = later.astype(BF16).T
 
     def turn_plane(a, _):
         turn(gp[a, 0:8], gwt, a * 256)
@@ -165,9 +178,14 @@
         )
         for tap in taps:
             piece = out[:, (tap - first) * 128 : (tap - first) * 128 + 128]
-            acc[tap * 192 + 64 : tap * 192 + 192] = piece[:128].T
-            acc[tap * 192 : tap * 192 + 64] = piece[128:].T[64:]
-
+            acc[first_row(tap) + 64 : first_row(tap) + 192] = piece[:128].T
+            acc[first_row(tap) : first_row(tap) + 64] = piece[128:].T[64:]
+
+    soon = remote(
+        acc.at[pl.ds(pl.multiple_of((1 - c) * 1344, CHUNK), EARLY)], pair_r.at[0:EARLY],
+        pair_sem.at[4], pair_sem.at[5], other,
+    )
+    soon.start()
     pl.semaphore_wait(know.at[0], 3)
     for device in along_x:
         pl.semaphore_signal(know.at[1], inc=1, device_id=device, device_id_type=MESH)
@@ -191,29 +209,29 @@
             piece = by_z[:, tap * 128 : tap * 128 + 128]
         else:
             piece = by_y[:, tap // 3 * 128 : tap // 3 * 128 + 128]
-        acc[tap * 192 + 64 : tap * 192 + 192] += piece[:128].T
-        acc[tap * 192 : tap * 192 + 64] += piece[128:].T[64:]
-
-    mine = pl.multiple_of(c * HALF, 8)
-    theirs = pl.multiple_of((1 - c) * HALF, 8)
-    swap = remote(acc.at[pl.ds(theirs, HALF)], pair_r, pair_sem.at[0], pair_sem.at[1], other)
+        acc[first_row(tap) + 64 : first_row(tap) + 192] += piece[:128].T
+        acc[first_row(tap) : first_row(tap) + 64] += piece[128:].T[64:]
+
+    mine = pl.multiple_of(c * HALF, CHUNK)
+    late = pl.multiple_of(EARLY + (1 - c) * LATE, CHUNK)
+    swap = remote(
+        acc.at[pl.ds(late, LATE)], pair_r.at[EARLY:HALF], pair_sem.at[0], pair_sem.at[1], other
+    )
     swap.start()
+    soon.wait_recv()
+    acc[pl.ds(pl.multiple_of(c * 1344, CHUNK), EARLY)] += pair_r[0:EARLY]
     swap.wait_recv()
-    acc[pl.ds(mine, HALF)] = acc[pl.ds(mine, HALF)] + pair_r[...]
+    acc[pl.ds(pl.multiple_of(EARLY + c * LATE, CHUNK), LATE)] += pair_r[EARLY:HALF]
 
     pl.semaphore_wait(know.at[1], 3)
 
-    def scatter(k, _):
-        j, device = peer(k)
+    for k, offset in enumerate(OFFSETS):
+        j, device = peer(offset)
 
         @pl.when(j < OWNERS)
         def _():
             row = pl.multiple_of(mine + j * CHUNK, CHUNK)
             remote(acc.at[pl.ds(row, CHUNK)], rs_r.at[k], rs_sem.at[0], rs_sem.at[1], device).start()
-
-        return 0
-
-    lax.fori_loop(0, PEERS, scatter, 0)
 
     def tap_rows(kz, ky):
         return wd[(kz * 3 + ky) * 128 : (kz * 3 + ky) * 128 + 128]
@@ -260,16 +278,13 @@
             if plane >= 0:
                 wide[a * 256 : a * 256 + 32, kz * 384 : kz * 384 + 128] = fy_r[plane] * y_on
 
-    def gather(k, _):
-        remote(ag.at[me], ag.at[me], ag_sem.at[0], ag_sem.at[1], peer(k)[1]).start()
-        return 0
-
     @pl.when(me < OWNERS)
     def _():
         pltpu.make_async_copy(rs_r, rs_r, rs_sem.at[1]).wait()
         own = acc[pl.ds(pl.multiple_of(mine + me * CHUNK, CHUNK), CHUNK)]
         ag[me] = (own + jnp.sum(rs_r[...], 0)).astype(BF16)
-        lax.fori_loop(0, PEERS, gather, 0)
+        for offset in OFFSETS:
+            remote(ag.at[me], ag.at[me], ag_sem.at[0], ag_sem.at[1], peer(offset)[1]).start()
 
     def forward(a, _):
         rows = pl.ds(pl.multiple_of(a * 256, 256), 256)
@@ -293,7 +308,17 @@
     trade = remote(ag, ag_x, pair_sem.at[2], pair_sem.at[3], other)
     trade.start()
 
+
+    def place(buffer, half):
+        for j in range(OWNERS):
+            row = half * HALF + j * CHUNK
+            row = jnp.where(row < 384, row + 768, jnp.where(row < 1152, row - 384, row))
+            kg[pl.ds(pl.multiple_of(row, CHUNK), CHUNK)] = buffer[j].astype(F32)
+
+    place(ag, c)
     trade.wait_recv()
+    place(ag_x, 1 - c)
+    soon.wait_send()
     swap.wait_send()
     trade.wait_send()
 
@@ -313,21 +338,13 @@
     co_out.wait()
 
 
-def finish_body(coarse, fgrad, ag, ag_x, coarse_out, fgrad_out, kgrad_out, kg_v, sem):
-    first = pltpu.make_async_copy(fgrad, fgrad_out, sem.at[0])
-    second = pltpu.make_async_copy(coarse, coarse_out, sem.at[1])
-    first.start()
-    second.start()
-    c = lax.axis_index("gz") & 1
-    for buffer, half in ((ag, c), (ag_x, 1 - c)):
-        for j in range(OWNERS):
-            row = pl.multiple_of(half * HALF + j * CHUNK, CHUNK)
-            kg_v[pl.ds(row, CHUNK)] = buffer[j].astype(F32)
-    third = pltpu.make_async_copy(kg_v, kgrad_out, sem.at[2])
-    third.start()
-    first.wait()
-    second.wait()
-    third.wait()
+def finish_body(*refs):
+    sem = refs[6]
+    copies = [pltpu.make_async_copy(refs[i], refs[i + 3], sem.at[i]) for i in (1, 2, 0)]
+    for copy in copies:
+        copy.start()
+    for copy in copies:
+        copy.wait()
 
 
 def shards(features, occupancy, kernel, upstream):
@@ -339,16 +356,16 @@
         jax.ShapeDtypeStruct((8, 8, 32, 128), BF16),
         jax.ShapeDtypeStruct((16, 16, 32, 128), BF16),
     )
-    gathered = jax.ShapeDtypeStruct((OWNERS, CHUNK, 128), BF16)
+    summed = jax.ShapeDtypeStruct((1728, 128), F32)
     arguments = [
         pltpu.with_memory_space_constraint(a, pltpu.HBM)
         for a in (features, occupancy, kernel, upstream)
     ]
     parts = pl.pallas_call(
         kernel_body,
-        out_shape=shapes + (gathered, gathered),
+        out_shape=shapes + (summed,),
         in_specs=[any_space] * 4,
-        out_specs=(any_space, any_space, in_vmem, in_vmem),
+        out_specs=(any_space, any_space, in_vmem),
         scratch_shapes=[
             vm((16, 16, 32, 128), BF16),
             vm((9, 9, 32, 128), BF16),
@@ -369,6 +386,8 @@
             vm((32, 128), BF16),
             vm((HALF, 128), F32),
             vm((PEERS, CHUNK, 128), F32),
+            vm((OWNERS, CHUNK, 128), BF16),
+            vm((OWNERS, CHUNK, 128), BF16),
             vm((8, 8, 32, 128), BF16),
             vm((16, 16, 32, 128), BF16),
             pltpu.SMEM((1, 1, 4), jnp.int32),
@@ -380,7 +399,7 @@
             dma((4,)),
             dma((6,)),
             dma((6,)),
-            dma((4,)),
+            dma((6,)),
             dma((2,)),
             dma((2,)),
             dma((2,)),
@@ -391,10 +410,10 @@
     )(*arguments)
     coarse, fgrad, kgrad = pl.pallas_call(
         finish_body,
-        out_shape=shapes + (jax.ShapeDtypeStruct((1728, 128), F32),),
-        in_specs=[any_space, any_space, in_vmem, in_vmem],
+        out_shape=shapes + (summed,),
+        in_specs=[any_space] * 3,
         out_specs=(any_space,) * 3,
-        scratch_shapes=[vm((1728, 128), F32), dma((3,))],
+        scratch_shapes=[dma((3,))],
         compiler_params=pltpu.CompilerParams(vmem_limit_bytes=4 * 1024 * 1024),
     )(*parts)
     return coarse, fgrad, kgrad.reshape(3, 3, 3, 64, 128)

time: 34.6 us -> 33.4 us (0.965)
  Pallas kernels: 33.8 us -> 32.7 us
    pallas_call x2, Pallas kernels: 33.8 us -> 32.7 us  [the longest x1 30.9 us: shards(): pl.pallas_call(kernel_body, out_shape=shapes + (summed,), in_specs=[any_s...]
where the time goes in v4:
time: 33.4 us; the launch traced here: 33.3 us
  Pallas kernels  32.7 us (98%)
  between operations  0.64 us (2%)
    pallas_call x1, Pallas kernels, shards(): pl.pallas_call(kernel_body, out_shape=shapes + (summed,), in_specs=[any_s...  30.9 us
    pallas_call x1, Pallas kernels, shards(): pl.pallas_call(finish_body, out_shape=shapes + (summed,), in_specs=[any_s...  1.8 us

profile of v4, /device:TPU:1, one launch (start us, length us, event | category | flops | bytes accessed | tf_op | source)
XLA Modules:
  0.0 33.3 jit_solution(14232496285898069621)
XLA Ops:
  0.6 30.9 %shard_map.67 = (bf16[8,8,32,128]{3,2,1,0:T(8,128)(2,1)S(1)}, bf16[16,16,32,128]{3,2,1,0:T(8,128)(2,1)S(1)}, f32[1728,128]{1,0:T(8,128)S(1)}) custom-call(bf16[16,16,32,128]{3,2,1,0:T(8,128)(2,1)} %feat.1, s32[1,1,4]{2,1,0:T(1,128)} %occ_h.1, bf16[3,3,3,64,128]{4,3,2,1,0:T(8,128)(2,1)} %ker.1, bf16[8,8,32,128]{3,2,1,0:T(8,128)(2,1)} %ups.1), custom_call_target="tpu_custom_call" | custom-call | tf_op jit(solution)/shard_map/pallas_call | solution.py:364
  31.5 1.8 %shard_map.68 = (bf16[8,8,32,128]{3,2,1,0:T(8,128)(2,1)}, bf16[16,16,32,128]{3,2,1,0:T(8,128)(2,1)}, f32[1728,128]{1,0:T(8,128)}) custom-call(bf16[8,8,32,128]{3,2,1,0:T(8,128)(2,1)S(1)} %get-tuple-element.9.refs_0_, bf16[16,16,32,128]{3,2,1,0:T(8,128)(2,1)S(1)} %get-tuple-element.10.refs_1_, f32[1728,128]{1,0:T(8,128)S(1)} %get-tuple-element.11.refs_2_), custom_call_target="tpu_custom_call" | custom-call | tf_op jit(solution)/shard_map/pallas_call | solution.py:411

commit v5 on v4

--- a/solution.py
+++ b/solution.py
@@ -54,8 +54,8 @@
     feat, occ_h, ker, ups, coarse, fgrad, kg,
     fv, gp, wv, mask, wide, gwt, wf, wd, acc,
     fz_s, fy_s, fz_r, fy_r, fc_r, gz_r, gy_r, gc_r,
-    pair_r, rs_r, ag, ag_x, co_v, fg_v, occ, gwz, rim_z,
-    gwy, rim_y, know, in_sem, hs_sem, hr_sem, pair_sem, rs_sem, ag_sem, out_sem,
+    pair_r, rs_r, ag, ag_x, occ, rim_zt, rim_z,
+    rim_yt, rim_y, know, in_sem, hs_sem, hr_sem, pair_sem, rs_sem, ag_sem,
 ):
     gz, gy = lax.axis_index("gz"), lax.axis_index("gy")
     x, y, z, c = coordinates()
@@ -150,6 +150,8 @@
             plane = 2 * a - 1 + kz
             edge = fy_s[plane] if plane >= 0 else jnp.zeros((32, 128), BF16)
             rim_y[a * 32 : a * 32 + 32, kz * 128 : kz * 128 + 128] = edge
+    rim_zt[...] = rim_z[...].T
+    rim_yt[...] = rim_y[...].T
 
     def widen(a, first):
         for kz in range(3):
@@ -197,20 +199,24 @@
     gp[8, 0:8] = gz_r[...] * last_z.astype(BF16)[None]
     gp[0:8, 8] = gy_r[...] * last_y.astype(BF16)[None]
     gp[8, 8] = gc_r[...] * (last_z * last_y).astype(BF16)
-    turn(gp[8, 0:8], gwz, 0)
-    turn(jnp.concatenate([gp[8, 8], jnp.zeros((96, 128), BF16)], 0), gwz, 256)
-    turn(gp[0:8, 8], gwy, 0)
-    by_z = jnp.dot(gwz[...], rim_z[...], preferred_element_type=F32)
-    by_y = jnp.dot(gwy[...], rim_y[...], preferred_element_type=F32)
+
+    def pairwise(flat):
+        place = lax.broadcasted_iota(jnp.int32, flat.shape, 0) % 32
+        later = jnp.where(place == 31, 0.0, pltpu.roll(flat.astype(F32), flat.shape[0] - 1, 0))
+        return jnp.concatenate([flat, later.astype(BF16)], 1)
+
+    beyond = [gp[8, 0:8].reshape(256, 128), gp[8, 8], jnp.zeros((96, 128), BF16)]
+    by_z = jnp.dot(rim_zt[...], pairwise(jnp.concatenate(beyond, 0)), preferred_element_type=F32)
+    by_y = jnp.dot(rim_yt[...], pairwise(gp[0:8, 8].reshape(256, 128)), preferred_element_type=F32)
     for tap in (0, 1, 2, 3, 6):
         if tap == 0:
-            piece = by_z[:, 0:128] + by_y[:, 0:128]
+            piece = by_z[0:128] + by_y[0:128]
         elif tap < 3:
-            piece = by_z[:, tap * 128 : tap * 128 + 128]
+            piece = by_z[tap * 128 : tap * 128 + 128]
         else:
-            piece = by_y[:, tap // 3 * 128 : tap // 3 * 128 + 128]
-        acc[first_row(tap) + 64 : first_row(tap) + 192] += piece[:128].T
-        acc[first_row(tap) : first_row(tap) + 64] += piece[128:].T[64:]
+            piece = by_y[tap // 3 * 128 : tap // 3 * 128 + 128]
+        acc[first_row(tap) + 64 : first_row(tap) + 192] += piece[:, :128]
+        acc[first_row(tap) : first_row(tap) + 64] += piece[64:, 128:]
 
     mine = pl.multiple_of(c * HALF, CHUNK)
     late = pl.multiple_of(EARLY + (1 - c) * LATE, CHUNK)
@@ -253,12 +259,10 @@
                 late = jnp.where(pair == 31, 0.0, pltpu.roll(d[:, 128:], 255, 0))
                 out = ((d[:, :128] + late) * mask[...]).astype(BF16)
                 for b in range(8):
-                    fg_v[2 * a + ez, 2 * b + ey] = out[b * 32 : b * 32 + 32]
+                    fgrad[2 * a + ez, 2 * b + ey] = out[b * 32 : b * 32 + 32]
         return 0
 
     lax.fori_loop(0, 8, back, 0)
-    fg_out = pltpu.make_async_copy(fg_v, fgrad, out_sem.at[0])
-    fg_out.start()
 
     for copy in halos[3:]:
         copy.wait_recv()
@@ -290,12 +294,10 @@
         rows = pl.ds(pl.multiple_of(a * 256, 256), 256)
         d = jnp.dot(wide[rows, :], wf[...], preferred_element_type=F32)
         late = jnp.where(pair == 0, 0.0, pltpu.roll(d[:, 128:], 1, 0))
-        co_v[a] = ((d[:, :128] + late) * mask[...]).astype(BF16).reshape(8, 32, 128)
+        coarse[a] = ((d[:, :128] + late) * mask[...]).astype(BF16).reshape(8, 32, 128)
         return 0
 
     lax.fori_loop(0, 8, forward, 0)
-    co_out = pltpu.make_async_copy(co_v, coarse, out_sem.at[1])
-    co_out.start()
 
     @pl.when(me < OWNERS)
     def _():
@@ -333,9 +335,6 @@
     def _():
         sent = rs_r.at[0:OWNERS]
         pltpu.make_async_copy(sent, sent, rs_sem.at[0]).wait()
-
-    fg_out.wait()
-    co_out.wait()
 
 
 def finish_body(*refs):
@@ -365,7 +364,7 @@
         kernel_body,
         out_shape=shapes + (summed,),
         in_specs=[any_space] * 4,
-        out_specs=(any_space, any_space, in_vmem),
+        out_specs=(in_vmem,) * 3,
         scratch_shapes=[
             vm((16, 16, 32, 128), BF16),
             vm((9, 9, 32, 128), BF16),
@@ -388,19 +387,16 @@
             vm((PEERS, CHUNK, 128), F32),
             vm((OWNERS, CHUNK, 128), BF16),
             vm((OWNERS, CHUNK, 128), BF16),
-            vm((8, 8, 32, 128), BF16),
-            vm((16, 16, 32, 128), BF16),
             pltpu.SMEM((1, 1, 4), jnp.int32),
-            vm((256, 384), BF16),
             vm((384, 384), BF16),
-            vm((256, 256), BF16),
+            vm((384, 384), BF16),
+            vm((384, 256), BF16),
             vm((256, 384), BF16),
             pltpu.SemaphoreType.REGULAR((2,)),
             dma((4,)),
             dma((6,)),
             dma((6,)),
             dma((6,)),
-            dma((2,)),
             dma((2,)),
             dma((2,)),
         ],

time: 33.4 us -> 33.3 us (level)
  no operation moved by 1% of the time
where the time goes in v5:
time: 33.3 us; the launch traced here: 33.2 us
  Pallas kernels  32.6 us (98%)
  between operations  0.64 us (2%)
    pallas_call x1, Pallas kernels, shards(): pl.pallas_call(kernel_body, out_shape=shapes + (summed,), in_specs=[any_s...  30.8 us
    pallas_call x1, Pallas kernels, shards(): pl.pallas_call(finish_body, out_shape=shapes + (summed,), in_specs=[any_s...  1.8 us

profile of v5, /device:TPU:1, one launch (start us, length us, event | category | flops | bytes accessed | tf_op | source)
XLA Modules:
  0.0 33.2 jit_solution(14028902465371065362)
XLA Ops:
  0.6 30.8 %shard_map.67 = (bf16[8,8,32,128]{3,2,1,0:T(8,128)(2,1)S(1)}, bf16[16,16,32,128]{3,2,1,0:T(8,128)(2,1)S(1)}, f32[1728,128]{1,0:T(8,128)S(1)}) custom-call(bf16[16,16,32,128]{3,2,1,0:T(8,128)(2,1)} %feat.1, s32[1,1,4]{2,1,0:T(1,128)} %occ_h.1, bf16[3,3,3,64,128]{4,3,2,1,0:T(8,128)(2,1)} %ker.1, bf16[8,8,32,128]{3,2,1,0:T(8,128)(2,1)} %ups.1), custom_call_target="tpu_custom_call" | custom-call | tf_op jit(solution)/shard_map/pallas_call | solution.py:363
  31.4 1.8 %shard_map.68 = (bf16[8,8,32,128]{3,2,1,0:T(8,128)(2,1)}, bf16[16,16,32,128]{3,2,1,0:T(8,128)(2,1)}, f32[1728,128]{1,0:T(8,128)}) custom-call(bf16[8,8,32,128]{3,2,1,0:T(8,128)(2,1)S(1)} %get-tuple-element.9.refs_0_, bf16[16,16,32,128]{3,2,1,0:T(8,128)(2,1)S(1)} %get-tuple-element.10.refs_1_, f32[1728,128]{1,0:T(8,128)S(1)} %get-tuple-element.11.refs_2_), custom_call_target="tpu_custom_call" | custom-call | tf_op jit(solution)/shard_map/pallas_call | solution.py:407

commit v6 on v5

--- a/solution.py
+++ b/solution.py
@@ -31,7 +31,11 @@
 
 
 def number(x, y, z):
-    return ((x * 16 + y * 4 + z) * 37) & 63
+    return number_of(x * 16 + y * 4 + z)
+
+
+def number_of(place):
+    return (place * 37) & 63
 
 
 def peer(offset):
@@ -55,11 +59,12 @@
     fv, gp, wv, mask, wide, gwt, wf, wd, acc,
     fz_s, fy_s, fz_r, fy_r, fc_r, gz_r, gy_r, gc_r,
     pair_r, rs_r, ag, ag_x, occ, rim_zt, rim_z,
-    rim_yt, rim_y, know, in_sem, hs_sem, hr_sem, pair_sem, rs_sem, ag_sem,
+    rim_yt, rim_y, know, in_sem, hs_sem, hr_sem, pair_sem, rs_sem, ag_sem, trade_sem,
 ):
     gz, gy = lax.axis_index("gz"), lax.axis_index("gy")
     x, y, z, c = coordinates()
     me = number(x, y, z)
+    slot = x * 16 + y * 4 + z
     other = (gz + 1 - 2 * c, gy)
     up, down = (gz + 1) % 32, (gz + 31) % 32
     nxt, prv = (gy + 1) % 4, (gy + 3) % 4
@@ -286,9 +291,10 @@
     def _():
         pltpu.make_async_copy(rs_r, rs_r, rs_sem.at[1]).wait()
         own = acc[pl.ds(pl.multiple_of(mine + me * CHUNK, CHUNK), CHUNK)]
-        ag[me] = (own + jnp.sum(rs_r[...], 0)).astype(BF16)
+        ag[slot] = (own + jnp.sum(rs_r[...], 0)).astype(BF16)
         for offset in OFFSETS:
-            remote(ag.at[me], ag.at[me], ag_sem.at[0], ag_sem.at[1], peer(offset)[1]).start()
+            landed = ag_sem.at[1 + (-offset[0]) % 4]
+            remote(ag.at[slot], ag.at[slot], ag_sem.at[0], landed, peer(offset)[1]).start()
 
     def forward(a, _):
         rows = pl.ds(pl.multiple_of(a * 256, 256), 256)
@@ -299,37 +305,55 @@
 
     lax.fori_loop(0, 8, forward, 0)
 
-    @pl.when(me < OWNERS)
-    def _():
-        pltpu.make_async_copy(ag.at[1:OWNERS], ag.at[1:OWNERS], ag_sem.at[1]).wait()
-
-    @pl.when(me >= OWNERS)
-    def _():
-        pltpu.make_async_copy(ag, ag, ag_sem.at[1]).wait()
-
-    trade = remote(ag, ag_x, pair_sem.at[2], pair_sem.at[3], other)
-    trade.start()
-
-
-    def place(buffer, half):
-        for j in range(OWNERS):
-            row = half * HALF + j * CHUNK
-            row = jnp.where(row < 384, row + 768, jnp.where(row < 1152, row - 384, row))
-            kg[pl.ds(pl.multiple_of(row, CHUNK), CHUNK)] = buffer[j].astype(F32)
-
-    place(ag, c)
-    trade.wait_recv()
-    place(ag_x, 1 - c)
+    for place in range(64):
+        if number_of(place) >= OWNERS:
+            ag[place] = jnp.zeros((CHUNK, 128), BF16)
+    trades = {}
+    for ahead in (0, 1, 3, 2):
+        group = (x + ahead) & 3
+        missing = group & 1
+        if ahead == 0:
+            missing = missing + jnp.where(me < OWNERS, 1, 0)
+        for count in (14, 13, 12):
+
+            @pl.when(missing == 14 - count)
+            def _():
+                part = ag.at[0:count]
+                pltpu.make_async_copy(part, part, ag_sem.at[1 + ahead]).wait()
+
+        rows = pl.ds(group * 16, 16)
+        trades[ahead] = remote(
+            ag.at[rows], ag_x.at[rows], trade_sem.at[ahead], trade_sem.at[4 + ahead], other
+        )
+        trades[ahead].start()
+
+    def write(buffer, half, places):
+        for which in range(2):
+
+            @pl.when(half == which)
+            def _():
+                for place in places:
+                    j = number_of(place)
+                    if j < OWNERS:
+                        row = which * HALF + j * CHUNK
+                        row = row + 768 if row < 384 else row - 384 if row < 1152 else row
+                        kg[row : row + CHUNK] = buffer[place].astype(F32)
+
+    write(ag, c, range(64))
+    for trade in trades.values():
+        trade.wait_recv()
+    write(ag_x, 1 - c, range(64))
     soon.wait_send()
     swap.wait_send()
-    trade.wait_send()
+    for trade in trades.values():
+        trade.wait_send()
 
     @pl.when(me < OWNERS)
     def _():
         sent = rs_r.at[1:OWNERS]
         pltpu.make_async_copy(sent, sent, rs_sem.at[0]).wait()
-        for part in (ag, ag.at[1 : PEERS - OWNERS + 1]):
-            pltpu.make_async_copy(part, part, ag_sem.at[0]).wait()
+        part = ag.at[0:PEERS]
+        pltpu.make_async_copy(part, part, ag_sem.at[0]).wait()
 
     @pl.when(me >= OWNERS)
     def _():
@@ -385,8 +409,8 @@
             vm((32, 128), BF16),
             vm((HALF, 128), F32),
             vm((PEERS, CHUNK, 128), F32),
-            vm((OWNERS, CHUNK, 128), BF16),
-            vm((OWNERS, CHUNK, 128), BF16),
+            vm((64, CHUNK, 128), BF16),
+            vm((64, CHUNK, 128), BF16),
             pltpu.SMEM((1, 1, 4), jnp.int32),
             vm((384, 384), BF16),
             vm((384, 384), BF16),
@@ -398,7 +422,8 @@
             dma((6,)),
             dma((6,)),
             dma((2,)),
-            dma((2,)),
+            dma((5,)),
+            dma((8,)),
         ],
         compiler_params=pltpu.CompilerParams(
             collective_id=0, has_side_effects=True, vmem_limit_bytes=48 * 1024 * 1024

time: 33.3 us -> 33.2 us (level)
  no operation moved by 1% of the time
where the time goes in v6:
time: 33.2 us; the launch traced here: 33 us
  Pallas kernels  32.4 us (98%)
  between operations  0.64 us (2%)
    pallas_call x1, Pallas kernels, shards(): pl.pallas_call(kernel_body, out_shape=shapes + (summed,), in_specs=[any_s...  30.6 us
    pallas_call x1, Pallas kernels, shards(): pl.pallas_call(finish_body, out_shape=shapes + (summed,), in_specs=[any_s...  1.8 us

profile of v6, /device:TPU:1, one launch (start us, length us, event | category | flops | bytes accessed | tf_op | source)
XLA Modules:
  0.0 33.0 jit_solution(9630048667371122264)
XLA Ops:
  0.6 30.6 %shard_map.67 = (bf16[8,8,32,128]{3,2,1,0:T(8,128)(2,1)S(1)}, bf16[16,16,32,128]{3,2,1,0:T(8,128)(2,1)S(1)}, f32[1728,128]{1,0:T(8,128)S(1)}) custom-call(bf16[16,16,32,128]{3,2,1,0:T(8,128)(2,1)} %feat.1, s32[1,1,4]{2,1,0:T(1,128)} %occ_h.1, bf16[3,3,3,64,128]{4,3,2,1,0:T(8,128)(2,1)} %ker.1, bf16[8,8,32,128]{3,2,1,0:T(8,128)(2,1)} %ups.1), custom_call_target="tpu_custom_call" | custom-call | tf_op jit(solution)/shard_map/pallas_call | solution.py:387
  31.2 1.8 %shard_map.68 = (bf16[8,8,32,128]{3,2,1,0:T(8,128)(2,1)}, bf16[16,16,32,128]{3,2,1,0:T(8,128)(2,1)}, f32[1728,128]{1,0:T(8,128)}) custom-call(bf16[8,8,32,128]{3,2,1,0:T(8,128)(2,1)S(1)} %get-tuple-element.9.refs_0_, bf16[16,16,32,128]{3,2,1,0:T(8,128)(2,1)S(1)} %get-tuple-element.10.refs_1_, f32[1728,128]{1,0:T(8,128)S(1)} %get-tuple-element.11.refs_2_), custom_call_target="tpu_custom_call" | custom-call | tf_op jit(solution)/shard_map/pallas_call | solution.py:432

commit v7 on v5

--- a/solution.py
+++ b/solution.py
@@ -312,10 +312,14 @@
 
 
     def place(buffer, half):
-        for j in range(OWNERS):
-            row = half * HALF + j * CHUNK
-            row = jnp.where(row < 384, row + 768, jnp.where(row < 1152, row - 384, row))
-            kg[pl.ds(pl.multiple_of(row, CHUNK), CHUNK)] = buffer[j].astype(F32)
+        for which in range(2):
+
+            @pl.when(half == which)
+            def _():
+                for j in range(OWNERS):
+                    row = which * HALF + j * CHUNK
+                    row = row + 768 if row < 384 else row - 384 if row < 1152 else row
+                    kg[row : row + CHUNK] = buffer[j].astype(F32)
 
     place(ag, c)
     trade.wait_recv()

time: 33.3 us -> 33.3 us (level)
  no operation moved by 1% of the time
where the time goes in v7:
time: 33.3 us; the launch traced here: 33.2 us
  Pallas kernels  32.5 us (98%)
  between operations  0.64 us (2%)
    pallas_call x1, Pallas kernels, shards(): pl.pallas_call(kernel_body, out_shape=shapes + (summed,), in_specs=[any_s...  30.7 us
    pallas_call x1, Pallas kernels, shards(): pl.pallas_call(finish_body, out_shape=shapes + (summed,), in_specs=[any_s...  1.8 us

profile of v7, /device:TPU:1, one launch (start us, length us, event | category | flops | bytes accessed | tf_op | source)
XLA Modules:
  0.0 33.2 jit_solution(10716495121594407072)
XLA Ops:
  0.6 30.7 %shard_map.67 = (bf16[8,8,32,128]{3,2,1,0:T(8,128)(2,1)S(1)}, bf16[16,16,32,128]{3,2,1,0:T(8,128)(2,1)S(1)}, f32[1728,128]{1,0:T(8,128)S(1)}) custom-call(bf16[16,16,32,128]{3,2,1,0:T(8,128)(2,1)} %feat.1, s32[1,1,4]{2,1,0:T(1,128)} %occ_h.1, bf16[3,3,3,64,128]{4,3,2,1,0:T(8,128)(2,1)} %ker.1, bf16[8,8,32,128]{3,2,1,0:T(8,128)(2,1)} %ups.1), custom_call_target="tpu_custom_call" | custom-call | tf_op jit(solution)/shard_map/pallas_call | solution.py:367
  31.4 1.8 %shard_map.68 = (bf16[8,8,32,128]{3,2,1,0:T(8,128)(2,1)}, bf16[16,16,32,128]{3,2,1,0:T(8,128)(2,1)}, f32[1728,128]{1,0:T(8,128)}) custom-call(bf16[8,8,32,128]{3,2,1,0:T(8,128)(2,1)S(1)} %get-tuple-element.9.refs_0_, bf16[16,16,32,128]{3,2,1,0:T(8,128)(2,1)S(1)} %get-tuple-element.10.refs_1_, f32[1728,128]{1,0:T(8,128)S(1)} %get-tuple-element.11.refs_2_), custom_call_target="tpu_custom_call" | custom-call | tf_op jit(solution)/shard_map/pallas_call | solution.py:411
